TPU v7x, 32 devices: a whole 2x2x4 slice. The times are simulated.
32 devices in a mesh: rep: 8 (over y, x, core), shard: 4 (over z).
Axes of the slice: x: 2, y: 2, z: 4, core: 2. Of those that a mesh axis runs over, the one named last changes fastest.
Arguments:
- tokens: bfloat16 [16384, 576], P(('rep', 'shard')), may hold values from -6 to 6
- lengths: int32 [32, 4], P(('rep', 'shard')), may hold values from 0 to 512, as said below
- gain_attn: bfloat16 [576], P('shard'), may hold values from 0.099609375 to 1.8984375
- w_query: bfloat16 [576, 576], P('shard'), may hold values from -0.25 to 0.25
- w_key: bfloat16 [576, 192], P('shard'), may hold values from -0.25 to 0.25
- w_value: bfloat16 [576, 192], P('shard'), may hold values from -0.25 to 0.25
- w_out: bfloat16 [576, 576], P('shard'), may hold values from -0.75 to 0.75
- gain_mlp: bfloat16 [576], P('shard'), may hold values from 0.099609375 to 1.8984375
- w_gate: bfloat16 [576, 1536], P('shard'), may hold values from -0.25 to 0.25
- w_up: bfloat16 [576, 1536], P('shard'), may hold values from -0.25 to 0.25
- w_down: bfloat16 [1536, 576], P('shard'), may hold values from -0.15625 to 0.15625
- cotangent: bfloat16 [16384, 576], P(('rep', 'shard')), may hold values from -6 to 6
Outputs:
- output: bfloat16 [16384, 576], P(('rep', 'shard'))
- grad_tokens: bfloat16 [16384, 576], P(('rep', 'shard'))
- grad_gain_attn: float32 [576], P('shard')
- grad_w_query: float32 [576, 576], P('shard')
- grad_w_key: float32 [576, 192], P('shard')
- grad_w_value: float32 [576, 192], P('shard')
- grad_w_out: float32 [576, 576], P('shard')
- grad_gain_mlp: float32 [576], P('shard')
- grad_w_gate: float32 [576, 1536], P('shard')
- grad_w_up: float32 [576, 1536], P('shard')
- grad_w_down: float32 [1536, 576], P('shard')
Inputs may be any that keep to these rules, and one draw needn't show every extreme that they name: Each slab's lengths sum to between 128 and 512; lengths may be 0; in every draw some slab holds one sequence of 512 tokens and nothing else.
All inputs are finite; a program needn't handle non-finite values.
Results may differ from a plain program's by a relative error of at most 0.015.
Values may be sent and summed in bfloat16 or wider, within the bound.
No kernel may reach another device: no remote copies, remote signals or barrier semaphores. Data moves between devices by JAX's collectives and lax.ppermute only.
A program may use at most 128 MiB of HBM per device.

v0:
```python
import functools

import jax
import jax.numpy as jnp
from jax import lax
from jax.experimental import pallas as pl
from jax.experimental.pallas import tpu as pltpu
from jax.sharding import PartitionSpec as P
import numpy as np

HEADS = 9
KV = 3
HD = 64
RATIO = HEADS // KV


norm_eps = 1e-05
rope_base = 100000.0
neg_fill = -1e30

low = jnp.bfloat16
f32 = jnp.float32
QUERY_ROWS = 128


def rotation_tables(places, head_size):
    half = head_size // 2
    freq = np.float32(rope_base) ** (-(np.arange(half, dtype=np.float32) * np.float32(2.0) / head_size))
    angle = np.arange(places, dtype=np.float32)[:, None] * freq.astype(np.float32)[None, :]
    return np.concatenate([np.cos(angle)] * 4, axis=1), np.concatenate([np.sin(angle)] * 4, axis=1)


def matmul(left, right):
    return jnp.dot(left, right, preferred_element_type=f32)


def matmul_left_t(left, right):
    return lax.dot_general(left, right, (((0,), (0,)), ((), ())), preferred_element_type=f32)


def matmul_right_t(left, right):
    return lax.dot_general(left, right, (((1,), (1,)), ((), ())), preferred_element_type=f32)


def flip(value, bit, replicas):
    return lax.ppermute(value, "rep", [(i, i ^ (1 << bit)) for i in range(replicas)])


def shift_from(value, step, shards):
    return lax.ppermute(value, "shard", [((s + step) % shards, s) for s in range(shards)])


def shift_to(value, step, shards):
    return lax.ppermute(value, "shard", [(s, (s + step) % shards) for s in range(shards)])


def add_low(left, right):
    return (left.astype(f32) + right.astype(f32)).astype(low)


def gather(mine, order, shards, replicas):
    got = jnp.stack([shift_from(mine, step, shards) for step in range(1, shards)])
    for bit in order[:-1]:
        got = jnp.stack([got, flip(got, bit, replicas)])
    return got, flip(got, order[-1], replicas)


def scatter_in_plane(keep, send, order, replicas):
    other = flip(send, order[0], replicas)
    for bit in order[1:]:
        send = add_low(keep[1], other[1])
        moved = flip(send, bit, replicas)
        keep = add_low(keep[0], other[0])
        other = moved
    return keep, other


def scatter_over_shards(keep, other, shards, replicas):
    parts = [add_low(keep[step], other[step]) for step in range(1, shards)]
    moved = [shift_to(part, step + 1, shards) for step, part in enumerate(parts)]
    total = keep[0].astype(f32) + other[0].astype(f32)
    for part in moved:
        total = total + part.astype(f32)
    total = total.astype(low)
    bit = 3
    while (1 << bit) < replicas:
        total = add_low(total, flip(total, bit, replicas))
        bit += 1
    return total


def spread(total, order, replicas):
    for bit in order[:-1]:
        total = jnp.stack([total, flip(total, bit, replicas)])
    return total, flip(total, order[-1], replicas)


class Copies:
    def __init__(self, sems):
        self.sems = sems
        self.made = []

    def start(self, source, target):
        copy = pltpu.make_async_copy(source, target, self.sems.at[len(self.made)])
        copy.start()
        self.made.append(copy)

    def wait(self):
        for copy in self.made:
            copy.wait()


def rows_at(start, count, unit=16):
    return pl.ds(pl.multiple_of(start, unit), count)


def relative(bit, rel):
    return 1 - bit if rel else bit


def shard_at(shard, step, shards):
    at = shard + step
    return jnp.where(at >= shards, at - shards, at)


def swap_halves(values):
    lane = lax.broadcasted_iota(jnp.int32, values.shape, 1)
    return jnp.where(
        lane % HD < HD // 2,
        pltpu.roll(values, 2 * HD - HD // 2, 1),
        pltpu.roll(values, HD // 2, 1),
    )


def norm_recip(values):
    return lax.rsqrt(jnp.mean(values * values, axis=-1, keepdims=True) + norm_eps)


def norm_back(values, recip, gain, grad_normed):
    scaled = grad_normed * gain
    inner = jnp.mean(scaled * values, axis=-1, keepdims=True)
    grad_values = recip * scaled - values * (recip * recip * recip * inner)
    grad_gain = jnp.sum(grad_normed * values * recip, axis=0, keepdims=True)
    return (grad_values, grad_gain)


def prepare_kernel(
    where_ref,
    lengths,
    tokens_t,
    cotangent_t,
    table_cos,
    table_sin,
    gate,
    up,
    down_t,
    cosine,
    sine,
    bias,
    hidden,
    scaled,
    grad_low,
    pair_mine,
    down_mine,
    down,
):
    core, x, y = (where_ref[i] for i in range(3))
    block = 2 * core + x
    columns = rows_at(384 * block, 384, 128)
    pair_mine[...] = jnp.where(y == 0, gate[:, columns], up[:, columns])
    down[...] = down_t[...].T
    eighth = down_mine.shape[0]
    down_mine[...] = down[rows_at(eighth * (2 * block + y), eighth), :]
    rows = hidden.shape[0]
    count = lengths.shape[1]
    ends = []
    for i in range(count):
        ends.append(lengths[0, i] + (ends[-1] if ends else 0))
    place = lax.broadcasted_iota(jnp.int32, cosine.shape, 0)
    start_cos = jnp.broadcast_to(table_cos[0:1], cosine.shape)
    start_sin = jnp.broadcast_to(table_sin[0:1], cosine.shape)
    for end in ends:
        start_cos = jnp.where(place >= end, table_cos[pl.ds(end, 1)], start_cos)
        start_sin = jnp.where(place >= end, table_sin[pl.ds(end, 1)], start_sin)
    cos, sin = table_cos[0:rows], table_sin[0:rows]
    cosine[...] = cos * start_cos + sin * start_sin
    signed = sin * start_cos - cos * start_sin
    lane = lax.broadcasted_iota(jnp.int32, cosine.shape, 1)
    sine[...] = jnp.where(lane % HD < HD // 2, -signed, signed)
    query = lax.broadcasted_iota(jnp.int32, bias.shape, 0)
    key = lax.broadcasted_iota(jnp.int32, bias.shape, 1)
    allowed = query >= key
    for end in ends:
        allowed = allowed & ((query < end) | (key >= end))
    bias[...] = jnp.where(allowed, 0.0, neg_fill)
    values = tokens_t[...].T.astype(f32)
    hidden[...] = values
    scaled[...] = values * norm_recip(values)
    wide = lax.broadcasted_iota(jnp.int32, grad_low.shape, 0)
    grad_low[...] = jnp.where(wide < ends[-1], cotangent_t[...].T, jnp.zeros((), low))


def project_kernel(
    shards,
    part,
    where_ref,
    scaled,
    cosine,
    sine,
    own,
    pieces,
    other,
    weights,
    gains,
    normed,
    query,
    keys,
    values,
    sems,
):
    core, x, y, shard = (where_ref[i] for i in range(4))
    width = scaled.shape[1]
    copies = Copies(sems)
    copies.start(own.at[pl.ds(0, part)], weights.at[rows_at(part * shard, part)])
    copies.start(own.at[pl.ds(part, 16)], weights.at[rows_at(width + 16 * shard, 16)])
    for rel_core, source in enumerate((pieces, other)):
        for rel_x in range(2):
            for rel_y in range(2):
                at_y = relative(y, rel_y)
                block = 2 * relative(core, rel_core) + relative(x, rel_x)
                columns = rows_at(384 * block, 384, 128)
                for step in range(1, shards):
                    at = shard_at(shard, step, shards)
                    piece = source.at[rel_x, rel_y, step - 1]
                    copies.start(
                        piece.at[pl.ds(0, 64)], weights.at[rows_at(part * at + 80 * at_y, 64), columns]
                    )
                    last = jnp.where(at_y == 0, part * at + 64, width + 16 * at)
                    copies.start(piece.at[pl.ds(64, 16)], weights.at[rows_at(last, 16), columns])
    copies.wait()
    total = sum(
        weights[width + 16 * s : width + 16 * s + 16, :width].astype(f32) for s in range(shards)
    )
    gains[...] = total[:8]
    n1 = (scaled[...] * total[0:1]).astype(low)
    normed[...] = n1
    for block in range(8):
        start = 512 + 128 * block
        result = matmul(n1, weights[0:width, start : start + 128])
        heads = [2 * block - 1, 2 * block]
        if heads[0] < HEADS + KV:
            turned = result * cosine[...] + swap_halves(result) * sine[...]
        for side, head in enumerate(heads):
            lanes = slice(HD * side, HD * side + HD)
            if head < 0:
                continue
            if head < HEADS:
                query[head] = (turned[:, lanes] * HD**-0.5).astype(low)
            elif head < HEADS + KV:
                keys[head - HEADS] = turned[:, lanes].astype(low)
            else:
                values[head - HEADS - KV] = result[:, lanes].astype(low)


def attend_kernel(kv, bias, query, keys, values, mixed, log_total):
    rows = bias.shape[0]
    for block in range(rows // QUERY_ROWS):
        at = slice(QUERY_ROWS * block, QUERY_ROWS * (block + 1))
        reach = QUERY_ROWS * (block + 1)
        stacked = jnp.concatenate([query[RATIO * kv + i, at] for i in range(RATIO)], axis=0)
        scores = matmul_right_t(stacked, keys[kv, :reach])
        logits = scores.reshape(RATIO, QUERY_ROWS, reach) + bias[at, :reach][None]
        top = jnp.max(logits, axis=-1, keepdims=True)
        expo = jnp.exp(logits - top)
        total = jnp.sum(expo, axis=-1, keepdims=True)
        probs = (expo * (1.0 / total)).astype(low).reshape(RATIO * QUERY_ROWS, reach)
        log_total[:, at] = top + jnp.log(total)
        result = matmul(probs, values[kv, :reach]).astype(low)
        for i in range(RATIO):
            mixed[at, HD * i : HD * i + HD] = result[QUERY_ROWS * i : QUERY_ROWS * (i + 1)]


def attend_last_kernel(
    kv,
    bias,
    query,
    keys,
    values,
    hidden_in,
    gains,
    weights,
    *rest,
):
    before, (mixed, log_total, hidden_one, normed_two) = rest[:kv], rest[kv:]
    attend_kernel(kv, bias, query, keys, values, mixed, log_total)
    width = hidden_in.shape[1]
    every = jnp.concatenate([item[...] for item in before] + [mixed[...]], axis=1)
    hidden = hidden_in[...] + matmul(every, weights[0:width, 0:width])
    hidden_one[...] = hidden
    normed_two[...] = (hidden * norm_recip(hidden) * gains[1:2]).astype(low)


def feed_kernel(
    shards,
    part,
    where_ref,
    hidden_one,
    normed_two,
    gains,
    lengths,
    cotangent,
    own_gate,
    own_up,
    own_down,
    pair_pieces,
    pair_other,
    down_pieces,
    down_other,
    result,
    grad_one,
    grad_gain,
    pair_keep,
    pair_send,
    down_keep,
    down_send,
    pair,
    down,
    hidden,
    grad_gate,
    grad_up,
    grad_pair,
    grad_down,
    sems,
):
    core, x, y, shard = (where_ref[i] for i in range(4))
    width = hidden_one.shape[1]
    down_part = own_down.shape[0]
    eighth = down_part // 8
    copies = Copies(sems)
    copies.start(own_gate, pair.at[0, rows_at(part * shard, part)])
    copies.start(own_up, pair.at[1, rows_at(part * shard, part)])
    copies.start(own_down, down.at[rows_at(down_part * shard, down_part)])
    for rel_core, (source, down_source) in enumerate(
        ((pair_pieces, down_pieces), (pair_other, down_other))
    ):
        at_core = relative(core, rel_core)
        for rel_x in range(2):
            at_x = relative(x, rel_x)
            block = 2 * at_core + at_x
            columns = rows_at(384 * block, 384, 128)
            for rel_y in range(2):
                at_y = relative(y, rel_y)
                for step in range(1, shards):
                    at = shard_at(shard, step, shards)
                    copies.start(
                        source.at[rel_x, rel_y, step - 1],
                        pair.at[at_y, rows_at(part * at, part), columns],
                    )
                    copies.start(
                        down_source.at[rel_y, rel_x, step - 1],
                        down.at[rows_at(down_part * at + eighth * (2 * block + at_y), eighth)],
                    )
    grad_low = cotangent[...]
    n2 = normed_two[...]
    copies.wait()
    hidden_width = pair.shape[2]
    for start in range(0, hidden_width, 384):
        at = slice(start, start + 384)
        gate = matmul(n2, pair[0, :, at])
        upward = matmul(n2, pair[1, :, at])
        grad_hidden = matmul_right_t(grad_low, down[at, :])
        sigma = jax.nn.sigmoid(gate)
        active = gate * sigma
        hidden[:, at] = (active * upward).astype(low)
        grad_up[:, at] = (grad_hidden * active).astype(low)
        grad_gate[:, at] = (grad_hidden * upward * (sigma + active * (1.0 - sigma))).astype(low)
    turned = n2.T
    sent = Copies(sems)
    for unit, grads in enumerate((grad_gate, grad_up)):
        for block in range(4):
            at = slice(384 * block, 384 * block + 384)
            grad_pair[unit, :, at] = matmul(turned, grads[:, at]).astype(low)
    for start in range(0, hidden_width, 384):
        at = slice(start, start + 384)
        grad_down[at, :] = matmul_left_t(hidden[:, at], grad_low).astype(low)
    for rel_core, (target, down_target) in enumerate(((pair_keep, down_keep), (pair_send, down_send))):
        at_core = relative(core, rel_core)
        for rel_x in range(2):
            at_x = relative(x, rel_x)
            block = 2 * at_core + at_x
            columns = rows_at(384 * block, 384, 128)
            for rel_y in range(2):
                at_y = relative(y, rel_y)
                for step in range(shards):
                    at = shard_at(shard, step, shards)
                    sent.start(
                        grad_pair.at[at_y, rows_at(part * at, part), columns],
                        target.at[rel_x, rel_y, step],
                    )
                    sent.start(
                        grad_down.at[rows_at(down_part * at + eighth * (2 * block + at_y), eighth)],
                        down_target.at[rel_y, rel_x, step],
                    )
    h1 = hidden_one[...]
    total = lengths[0, 0]
    for i in range(1, lengths.shape[1]):
        total = total + lengths[0, i]
    row = lax.broadcasted_iota(jnp.int32, h1.shape, 0)
    summed = h1 + matmul(hidden[...], down[...])
    result[...] = jnp.where(row < total, summed, 0.0).astype(low).T
    grad_normed = matmul_right_t(grad_gate[...], pair[0]) + matmul_right_t(grad_up[...], pair[1])
    grad_from, gain_row = norm_back(h1, norm_recip(h1), gains[1:2], grad_normed)
    grad_one[...] = grad_low.astype(f32) + grad_from
    grad_gain[...] = jnp.broadcast_to(gain_row, grad_gain.shape)
    sent.wait()


def back_heads_kernel(
    kv,
    bias,
    cosine,
    sine,
    weights,
    query,
    keys,
    values,
    mixed,
    log_total,
    grad_one,
    grad_turned,
    grad_values_out,
    grad_out,
    grad_mixed,
    grad_heads,
):
    rows, width = grad_one.shape
    span = RATIO * HD
    da = grad_one[...].astype(low)
    grad_mixed[...] = matmul_right_t(da, weights[span * kv : span * kv + span, 0:width]).astype(low)
    grad_out[...] = matmul_left_t(mixed[...], da).astype(low)
    grad_keys = [None] * (rows // QUERY_ROWS)
    grad_values = [None] * (rows // QUERY_ROWS)
    for block in range(rows // QUERY_ROWS):
        at = slice(QUERY_ROWS * block, QUERY_ROWS * (block + 1))
        reach = QUERY_ROWS * (block + 1)
        stacked = jnp.concatenate([query[RATIO * kv + i, at] for i in range(RATIO)], axis=0)
        grads = jnp.concatenate([grad_mixed[at, HD * i : HD * i + HD] for i in range(RATIO)], axis=0)
        out = jnp.concatenate([mixed[at, HD * i : HD * i + HD] for i in range(RATIO)], axis=0)
        delta = jnp.sum(grads.astype(f32) * out.astype(f32), axis=-1, keepdims=True)
        scores = matmul_right_t(stacked, keys[kv, :reach]).reshape(RATIO, QUERY_ROWS, reach)
        probs = jnp.exp(scores + bias[at, :reach][None] - log_total[:, at]).reshape(-1, reach)
        grad_probs = matmul_right_t(grads, values[kv, :reach])
        grad_scores = (probs * (grad_probs - delta)).astype(low)
        grad_query = matmul(grad_scores, keys[kv, :reach])
        for i in range(RATIO):
            grad_heads[at, HD * i : HD * i + HD] = (
                grad_query[QUERY_ROWS * i : QUERY_ROWS * (i + 1)] * HD**-0.5
            )
        key_part = matmul_left_t(grad_scores, stacked)
        value_part = matmul_left_t(probs.astype(low), grads)
        for j in range(block + 1):
            at_j = slice(QUERY_ROWS * j, QUERY_ROWS * (j + 1))
            if grad_keys[j] is None:
                grad_keys[j], grad_values[j] = key_part[at_j], value_part[at_j]
            else:
                grad_keys[j] = grad_keys[j] + key_part[at_j]
                grad_values[j] = grad_values[j] + value_part[at_j]
    grad_heads[:, span : span + HD] = jnp.concatenate(grad_keys, axis=0)
    grad_values_out[...] = jnp.concatenate(grad_values, axis=0).astype(low)
    for start in range(0, span + HD, 2 * HD):
        value = grad_heads[:, start : start + 2 * HD]
        turned = value * cosine[...] - swap_halves(value) * sine[...]
        grad_turned[:, start : start + 2 * HD] = turned.astype(low)


def back_last_kernel(
    shards,
    part,
    where_ref,
    hidden_in,
    gains,
    weights,
    normed,
    grad_one,
    grad_gain_two,
    *rest,
):
    core, x, y, shard = (where_ref[i] for i in range(4))
    rows, width = hidden_in.shape
    turned, values, outs = rest[0:KV], rest[KV : 2 * KV], rest[2 * KV : 3 * KV]
    grad_tokens, keep, send, grad_low, grad_weights, sems = rest[3 * KV :]
    span = RATIO * HD
    grad_low[...] = jnp.concatenate(
        [jnp.zeros((rows, HD), low)]
        + [item[:, 0:span] for item in turned]
        + [item[:, span : span + HD] for item in turned]
        + [item[...] for item in values],
        axis=1,
    )
    normed_t = normed[...].T
    for start in range(0, 1024, 512):
        at = slice(start, start + 512)
        grad_weights[0:width, 512 + start : 1024 + start] = matmul(normed_t, grad_low[:, at]).astype(low)
    for kv in range(KV):
        grad_weights[span * kv : span * kv + span, 0:width] = outs[kv][...]
    grad_normed = matmul_right_t(grad_low[...], weights[0:width, 512:1536])
    hidden = hidden_in[...]
    grad_from, gain_row = norm_back(hidden, norm_recip(hidden), gains[0:1], grad_normed)
    grad_tokens[...] = (grad_one[...] + grad_from).astype(low).T
    row = lax.broadcasted_iota(jnp.int32, (16, width), 0)
    both = jnp.where(
        row == 0,
        jnp.broadcast_to(gain_row, (16, width)),
        jnp.where(row == 1, jnp.broadcast_to(grad_gain_two[0:1], (16, width)), 0.0),
    )
    grad_weights[width : width + 16, :] = jnp.zeros((16, grad_weights.shape[1]), low)
    grad_weights[width : width + 16, 0:width] = both.astype(low)
    copies = Copies(sems)
    for rel_core, target in enumerate((keep, send)):
        for rel_x in range(2):
            for rel_y in range(2):
                at_y = relative(y, rel_y)
                block = 2 * relative(core, rel_core) + relative(x, rel_x)
                columns = rows_at(384 * block, 384, 128)
                for step in range(shards):
                    at = shard_at(shard, step, shards)
                    piece = target.at[rel_y, rel_x, step]
                    copies.start(
                        grad_weights.at[rows_at(part * at + 80 * at_y, 64), columns],
                        piece.at[pl.ds(0, 64)],
                    )
                    last = jnp.where(at_y == 0, part * at + 64, width)
                    copies.start(grad_weights.at[rows_at(last, 16), columns], piece.at[pl.ds(64, 16)])
    copies.wait()


def finish_feed_kernel(
    where_ref,
    pair_pieces,
    pair_other,
    down_pieces,
    down_other,
    out_gate,
    out_up,
    out_down,
    pair,
    down,
    sems,
):
    core, x, y = (where_ref[i] for i in range(3))
    eighth = down.shape[0] // 8
    copies = Copies(sems)
    for rel_core, (p_from, d_from) in enumerate(
        ((pair_pieces, down_pieces), (pair_other, down_other))
    ):
        for rel_x in range(2):
            for rel_y in range(2):
                at_y = relative(y, rel_y)
                block = 2 * relative(core, rel_core) + relative(x, rel_x)
                columns = rows_at(384 * block, 384, 128)
                copies.start(p_from.at[rel_x, rel_y], pair.at[at_y, :, columns])
                copies.start(
                    d_from.at[rel_y, rel_x], down.at[rows_at(eighth * (2 * block + at_y), eighth)]
                )
    copies.wait()
    out_gate[...] = pair[0].astype(f32)
    out_up[...] = pair[1].astype(f32)
    out_down[...] = down[...].T.astype(f32)


def finish_attn_kernel(
    where_ref,
    pieces,
    other,
    out_query,
    out_key,
    out_value,
    out_out,
    out_gains,
    attn,
    sems,
):
    core, x, y = (where_ref[i] for i in range(3))
    part = out_out.shape[0]
    copies = Copies(sems)
    for rel_core, source in enumerate((pieces, other)):
        for rel_x in range(2):
            for rel_y in range(2):
                block = 2 * relative(core, rel_core) + relative(x, rel_x)
                columns = rows_at(384 * block, 384, 128)
                copies.start(
                    source.at[rel_y, rel_x], attn.at[rows_at(80 * relative(y, rel_y), 80), columns]
                )
    copies.wait()
    width = out_out.shape[1]
    kv_width = out_key.shape[1]
    out_out[...] = attn[0:part, 0:width].astype(f32)
    rest = attn[0:part, 512:].astype(f32)
    at = width - 512
    out_query[...] = rest[:, at : at + width]
    out_key[...] = rest[:, at + width : at + width + kv_width]
    out_value[...] = rest[:, at + width + kv_width :]
    out_gains[...] = attn[part : part + 16, 0:width].astype(f32)[:8]


VM = pl.BlockSpec(memory_space=pltpu.VMEM)
SM = pl.BlockSpec(memory_space=pltpu.SMEM)
HB = pl.BlockSpec(memory_space=pl.ANY)


def shape(sizes, kind):
    return jax.ShapeDtypeStruct(tuple(sizes), kind)


def call(kernel, name, operands, in_specs, out_shape, out_specs, scratch, micros, room):
    moved = sum(item.size * item.dtype.itemsize for item in out_shape)
    return pl.pallas_call(
        kernel,
        name=name,
        in_specs=in_specs,
        out_shape=out_shape,
        out_specs=out_specs,
        scratch_shapes=scratch,
        cost_estimate=pl.CostEstimate(
            flops=int(micros * 1.1e9), bytes_accessed=moved, transcendentals=0
        ),
        compiler_params=pltpu.CompilerParams(vmem_limit_bytes=room << 20),
    )(*operands)


def local(
    replicas,
    shards,
    tokens,
    lengths,
    gain_attn,
    w_query,
    w_key,
    w_value,
    w_out,
    gain_mlp,
    w_gate,
    w_up,
    w_down,
    cotangent,
):
    rows, width = tokens.shape
    part = w_gate.shape[0]
    hidden_width = w_gate.shape[1]
    down_part = w_down.shape[0]
    eighth = down_part // 8
    packed = 2 * width + 2 * w_key.shape[1]
    rep_index = lax.axis_index("rep")
    shard = lax.axis_index("shard")
    core, x, y = ((rep_index >> bit) & 1 for bit in range(3))
    where = jnp.stack([core, x, y, shard]).astype(jnp.int32)
    block = 2 * core + x

    gain_rows = jnp.zeros((2, packed), low)
    gain_rows = lax.dynamic_update_slice(
        gain_rows, jnp.stack([gain_attn, gain_mlp]), (0, part * shard)
    )
    own = jnp.concatenate(
        [
            jnp.concatenate([w_out, w_query, w_key, w_value], axis=1),
            gain_rows,
            jnp.zeros((14, packed), low),
        ],
        axis=0,
    )
    attn_mine = lax.dynamic_slice(own, (80 * y, 384 * block), (80, 384))
    attn_got, attn_other = gather(attn_mine, (2, 1, 0), shards, replicas)
    table_cos, table_sin = rotation_tables(rows + 8, HD)
    cosine, sine, bias, hidden_in, scaled, grad_low, pair_mine, down_mine, own_down = call(
        prepare_kernel,
        "prepare",
        (where, lengths, tokens.T, cotangent.T, table_cos, table_sin, w_gate, w_up, w_down.T),
        [SM, SM] + [VM] * 7,
        (
            shape((rows, 2 * HD), f32),
            shape((rows, 2 * HD), f32),
            shape((rows, rows), f32),
            shape((rows, width), f32),
            shape((rows, width), f32),
            shape((rows, width), low),
            shape((part, 384), low),
            shape((eighth, width), low),
            shape((down_part, width), low),
        ),
        [VM] * 9,
        [],
        5,
        24,
    )
    pair_got, pair_other = gather(pair_mine, (2, 1, 0), shards, replicas)
    down_got, down_other = gather(down_mine, (1, 2, 0), shards, replicas)

    weights, gains, normed, query, keys, values = call(
        functools.partial(project_kernel, shards, part),
        "project",
        (where, scaled, cosine, sine, own, attn_got, attn_other),
        [SM, VM, VM, VM, HB, HB, HB],
        (
            shape((width + 16 * shards, packed), low),
            shape((8, width), f32),
            shape((rows, width), low),
            shape((HEADS, rows, HD), low),
            shape((KV, rows, HD), low),
            shape((KV, rows, HD), low),
        ),
        [VM] * 6,
        [pltpu.SemaphoreType.DMA((2 + 16 * (shards - 1),))],
        5,
        24,
    )
    mixed, log_total = [], []
    for kv in range(KV):
        outs = [shape((rows, RATIO * HD), low), shape((RATIO, rows, 1), f32)]
        operands = (bias, query, keys, values)
        if kv < KV - 1:
            one, two = call(
                functools.partial(attend_kernel, kv),
                f"attend_{kv}",
                operands,
                [VM] * 4,
                outs,
                [VM] * 2,
                [],
                3,
                24,
            )
        else:
            operands += (hidden_in, gains, weights, *mixed)
            one, two, hidden_one, normed_two = call(
                functools.partial(attend_last_kernel, kv),
                f"attend_{kv}",
                operands,
                [VM] * len(operands),
                outs + [shape((rows, width), f32), shape((rows, width), low)],
                [VM] * 4,
                [],
                4,
                24,
            )
        mixed.append(one)
        log_total.append(two)
    pair_shape = shape((2, 2, shards, part, 384), low)
    down_shape = shape((2, 2, shards, eighth, width), low)
    result, grad_one, grad_gain_two, pair_keep, pair_send, down_keep, down_send = call(
        functools.partial(feed_kernel, shards, part),
        "feed",
        (
            where,
            hidden_one,
            normed_two,
            gains,
            lengths,
            grad_low,
            w_gate,
            w_up,
            own_down,
            pair_got,
            pair_other,
            down_got,
            down_other,
        ),
        [SM] + [VM] * 3 + [SM, VM] + [HB] * 7,
        (
            shape((width, rows), low),
            shape((rows, width), f32),
            shape((8, width), f32),
            pair_shape,
            pair_shape,
            down_shape,
            down_shape,
        ),
        [VM] * 3 + [HB] * 4,
        [
            pltpu.VMEM((2, shards * part, hidden_width), low),
            pltpu.VMEM((hidden_width, width), low),
            pltpu.VMEM((rows, hidden_width), low),
            pltpu.VMEM((rows, hidden_width), low),
            pltpu.VMEM((rows, hidden_width), low),
            pltpu.VMEM((2, shards * part, hidden_width), low),
            pltpu.VMEM((hidden_width, width), low),
            pltpu.SemaphoreType.DMA((16 * shards + 3,)),
        ],
        19,
        48,
    )
    grad_turned, grad_values, grad_out = [], [], []
    for kv in range(KV):
        one, two, three = call(
            functools.partial(back_heads_kernel, kv),
            f"back_{kv}",
            (bias, cosine, sine, weights, query, keys, values, mixed[kv], log_total[kv], grad_one),
            [VM] * 10,
            (
                shape((rows, RATIO * HD + HD), low),
                shape((rows, HD), low),
                shape((RATIO * HD, width), low),
            ),
            [VM] * 3,
            [pltpu.VMEM((rows, RATIO * HD), low), pltpu.VMEM((rows, RATIO * HD + HD), f32)],
            5,
            24,
        )
        grad_turned.append(one)
        grad_values.append(two)
        grad_out.append(three)
    attn_shape = shape((2, 2, shards, 80, 384), low)
    grad_tokens, attn_keep, attn_send = call(
        functools.partial(back_last_kernel, shards, part),
        "back_last",
        (
            where,
            hidden_in,
            gains,
            weights,
            normed,
            grad_one,
            grad_gain_two,
            *grad_turned,
            *grad_values,
            *grad_out,
        ),
        [SM] + [VM] * (6 + 3 * KV),
        (shape((width, rows), low), attn_shape, attn_shape),
        [VM, HB, HB],
        [
            pltpu.VMEM((rows, 1024), low),
            pltpu.VMEM((width + 16, packed), low),
            pltpu.SemaphoreType.DMA((16 * shards,)),
        ],
        6,
        24,
    )
    pair_total = scatter_over_shards(
        *scatter_in_plane(pair_keep, pair_send, (0, 1, 2), replicas), shards, replicas
    )
    down_total = scatter_over_shards(
        *scatter_in_plane(down_keep, down_send, (0, 2, 1), replicas), shards, replicas
    )
    attn_total = scatter_over_shards(
        *scatter_in_plane(attn_keep, attn_send, (0, 2, 1), replicas), shards, replicas
    )
    g_gate, g_up, g_down = call(
        finish_feed_kernel,
        "finish_feed",
        (
            where,
            *spread(pair_total, (2, 1, 0), replicas),
            *spread(down_total, (1, 2, 0), replicas),
        ),
        [SM] + [HB] * 4,
        (
            shape(w_gate.shape, f32),
            shape(w_up.shape, f32),
            shape((width, down_part), f32),
        ),
        [VM] * 3,
        [
            pltpu.VMEM((2, part, hidden_width), low),
            pltpu.VMEM(w_down.shape, low),
            pltpu.SemaphoreType.DMA((16,)),
        ],
        3,
        16,
    )
    g_query, g_key, g_value, g_out, g_gains = call(
        finish_attn_kernel,
        "finish_attn",
        (where, *spread(attn_total, (1, 2, 0), replicas)),
        [SM] + [HB] * 2,
        (
            shape(w_query.shape, f32),
            shape(w_key.shape, f32),
            shape(w_value.shape, f32),
            shape(w_out.shape, f32),
            shape((8, width), f32),
        ),
        [VM] * 5,
        [pltpu.VMEM((160, packed), low), pltpu.SemaphoreType.DMA((8,))],
        2,
        16,
    )
    g_gains = lax.dynamic_slice(g_gains, (0, part * shard), (2, part))
    return (
        result.T,
        grad_tokens.T,
        g_gains[0],
        g_query,
        g_key,
        g_value,
        g_out,
        g_gains[1],
        g_gate,
        g_up,
        g_down.T,
    )


def solution(mesh):
    in_specs = (
        P(("rep", "shard"), None),
        P(("rep", "shard"), None),
        P("shard"),
        P("shard", None),
        P("shard", None),
        P("shard", None),
        P("shard", None),
        P("shard"),
        P("shard", None),
        P("shard", None),
        P("shard", None),
        P(("rep", "shard"), None),
    )
    out_specs = (
        P(("rep", "shard"), None),
        P(("rep", "shard"), None),
        P("shard"),
        P("shard", None),
        P("shard", None),
        P("shard", None),
        P("shard", None),
        P("shard"),
        P("shard", None),
        P("shard", None),
        P("shard", None),
    )
    part = functools.partial(local, mesh.shape["rep"], mesh.shape["shard"])
    return jax.shard_map(part, mesh=mesh, in_specs=in_specs, out_specs=out_specs, check_vma=False)
```

profile of v0, /device:TPU:0, one launch (start us, length us, event | category | flops | bytes accessed | tf_op | source)
XLA Modules:
  0.0 188.4 jit_solution(7043897254747725519)
XLA Ops:
  0.7 0.8 stack.173
  1.5 0.7 stack.174
  2.4 1.3 concatenate.6
  3.9 3.2 %collective-permute-start.2 = (bf16[80,384]{1,0:T(8,128)(2,1)S(1)}, bf16[80,384]{1,0:T(8,128)(2,1)S(1)}, u32[]{:S(2)}, u32[]{:S(2)}) collective-permute-start(bf16[80,384]{1,0:T(8,128)(2,1)S(1)} %dynamic_slice.6), channel_id=1, source_target_pairs={{3,0},{0,1},{1,2},{2,3},{7,4},{4,5},{5,6},{6,7},{11,8},{8,9},{9,10... | collective-permute-start | bytes 184328 | tf_op jit(solution)/shard_map/ppermute | solution.py:50
  7.1 2.6 %collective-permute-start.1 = (bf16[80,384]{1,0:T(8,128)(2,1)S(1)}, bf16[80,384]{1,0:T(8,128)(2,1)S(1)}, u32[]{:S(2)}, u32[]{:S(2)}) collective-permute-start(bf16[80,384]{1,0:T(8,128)(2,1)S(1)} %dynamic_slice.6), channel_id=1, source_target_pairs={{2,0},{3,1},{0,2},{1,3},{6,4},{7,5},{4,6},{5,7},{10,8},{11,9},{8,1... | collective-permute-start | bytes 184328 | tf_op jit(solution)/shard_map/ppermute | solution.py:50
  9.7 1.3 collective-permute-start
  11.2 1.0 copy-done.4
  12.2 0.9 copy-done.7
  13.1 0.9 copy-done.8
  14.1 1.7 prepare.1
  15.8 0.7 collective-permute-start.8
  16.9 2.8 %collective-permute-start.6 = (bf16[144,384]{1,0:T(8,128)(2,1)S(1)}, bf16[144,384]{1,0:T(8,128)(2,1)S(1)}, u32[]{:S(2)}, u32[]{:S(2)}) collective-permute-start(bf16[144,384]{1,0:T(8,128)(2,1)S(1)} %get-tuple-element.77), channel_id=1, source_target_pairs={{1,0},{2,1},{3,2},{0,3},{5,4},{6,5},{7,6},{4,7},{9,8},{10,9},{11,1... | collective-permute-start | bytes 331784 | tf_op jit(solution)/shard_map/ppermute | solution.py:50
  19.7 1.6 collective-permute-start.3
  21.3 2.4 %collective-permute-done.8 = bf16[144,384]{1,0:T(8,128)(2,1)S(1)} collective-permute-done((bf16[144,384]{1,0:T(8,128)(2,1)S(1)}, bf16[144,384]{1,0:T(8,128)(2,1)S(1)}, u32[]{:S(2)}, u32[]{:S(2)}) %collective-permute-start.8) | collective-permute-done | bytes 110624 | tf_op jit(solution)/shard_map/ppermute | solution.py:50
  23.7 2.8 %collective-permute-done.7 = bf16[144,384]{1,0:T(8,128)(2,1)S(1)} collective-permute-done((bf16[144,384]{1,0:T(8,128)(2,1)S(1)}, bf16[144,384]{1,0:T(8,128)(2,1)S(1)}, u32[]{:S(2)}, u32[]{:S(2)}) %collective-permute-start.7) | collective-permute-done | bytes 110624 | tf_op jit(solution)/shard_map/ppermute | solution.py:50
  26.6 1.6 collective-permute-start.9
  28.3 1.6 collective-permute-start.4
  29.9 2.3 %collective-permute-start.14 = (bf16[48,576]{1,0:T(8,128)(2,1)S(1)}, bf16[48,576]{1,0:T(8,128)(2,1)S(1)}, u32[]{:S(2)}, u32[]{:S(2)}) collective-permute-start(bf16[48,576]{1,0:T(8,128)(2,1)S(1)} %get-tuple-element.78), channel_id=1, source_target_pairs={{3,0},{0,1},{1,2},{2,3},{7,4},{4,5},{5,6},{6,7},{11,8},{8,9},{9,10... | collective-permute-start | bytes 165896 | tf_op jit(solution)/shard_map/ppermute | solution.py:50
  32.7 2.3 %collective-permute-start.12 = (bf16[48,576]{1,0:T(8,128)(2,1)S(1)}, bf16[48,576]{1,0:T(8,128)(2,1)S(1)}, u32[]{:S(2)}, u32[]{:S(2)}) collective-permute-start(bf16[48,576]{1,0:T(8,128)(2,1)S(1)} %get-tuple-element.78), channel_id=1, source_target_pairs={{1,0},{2,1},{3,2},{0,3},{5,4},{6,5},{7,6},{4,7},{9,8},{10,9},{11,1... | collective-permute-start | bytes 165896 | tf_op jit(solution)/shard_map/ppermute | solution.py:50
  35.0 1.0 collective-permute-done.14
  36.0 2.0 %collective-permute-done.13 = bf16[48,576]{1,0:T(8,128)(2,1)S(1)} collective-permute-done((bf16[48,576]{1,0:T(8,128)(2,1)S(1)}, bf16[48,576]{1,0:T(8,128)(2,1)S(1)}, u32[]{:S(2)}, u32[]{:S(2)}) %collective-permute-start.13) | collective-permute-done | bytes 55328 | tf_op jit(solution)/shard_map/ppermute | solution.py:50
  38.8 1.6 collective-permute-start.10
  40.6 5.2 %collective-permute-done.15 = bf16[3,48,576]{2,1,0:T(8,128)(2,1)S(1)} collective-permute-done((bf16[3,48,576]{2,1,0:T(8,128)(2,1)S(1)}, bf16[3,48,576]{2,1,0:T(8,128)(2,1)S(1)}, u32[]{:S(2)}, u32[]{:S(2)}) %collective-permute-start.15) | collective-permute-done | bytes 165920 | tf_op jit(solution)/shard_map/ppermute | solution.py:46
  46.4 7.0 %collective-permute-done.16 = bf16[2,3,48,576]{3,2,1,0:T(8,128)(2,1)S(1)} collective-permute-done((bf16[2,3,48,576]{3,2,1,0:T(8,128)(2,1)S(1)}, bf16[2,3,48,576]{3,2,1,0:T(8,128)(2,1)S(1)}, u32[]{:S(2)}, u32[]{:S(2)}) %collective-permute-start.16) | collective-permute-done | bytes 331808 | tf_op jit(solution)/shard_map/ppermute | solution.py:46
  53.6 3.5 %collective-permute-done.10 = bf16[2,3,144,384]{3,2,1,0:T(8,128)(2,1)S(1)} collective-permute-done((bf16[2,3,144,384]{3,2,1,0:T(8,128)(2,1)S(1)}, bf16[2,3,144,384]{3,2,1,0:T(8,128)(2,1)S(1)}, u32[]{:S(2)}, u32[]{:S(2)}) %collective-permute-start.10) | collective-permute-done | bytes 663584 | tf_op jit(solution)/shard_map/ppermute | solution.py:46
  57.4 3.8 %project.1 = (bf16[640,1536]{1,0:T(8,128)(2,1)S(1)}, f32[8,576]{1,0:T(8,128)S(1)}, bf16[512,576]{1,0:T(8,128)(2,1)S(1)}, bf16[9,512,64]{2,1,0:T(8,128)(2,1)S(1)}...) custom-call(s32[4]{0:T(128)S(1)} %pad_add_fusion.where_ref, f32[512,576]{1,0:T(8,128)S(1)} %get-tuple-element.62.scaled, ...), custom_call_target="tpu_custom_call" | custom-call | flops 5500000256 | bytes 3557376 | tf_op jit(solution)/shard_map/project/pallas_call | solution.py:617
  61.2 1.9 %attend_1.1 = (bf16[512,192]{1,0:T(8,128)(2,1)S(1)}, f32[3,512,1]{2,1,0:T(8,128)S(1)}) custom-call(f32[512,512]{1,0:T(8,128)S(1)} %get-tuple-element.61.bias, bf16[9,512,64]{2,1,0:T(8,128)(2,1)S(1)} %get-tuple-element.65.query, bf16[3,512,64]{2,1,0:T(8,128)(2,1)S(1)} %get-tuple-element.66.keys, bf16[3,512,64]{2,1,0:T(8,128)(2,1)S(1)} %get-tuple-element.67.values), custom_call_target="tpu_custom_call" | custom-call | flops 3300000000 | bytes 202752 | tf_op jit(solution)/shard_map/attend_1/pallas_call | solution.py:617
  63.2 1.9 %attend_0.1 = (bf16[512,192]{1,0:T(8,128)(2,1)S(1)}, f32[3,512,1]{2,1,0:T(8,128)S(1)}) custom-call(f32[512,512]{1,0:T(8,128)S(1)} %get-tuple-element.61.bias, bf16[9,512,64]{2,1,0:T(8,128)(2,1)S(1)} %get-tuple-element.65.query, bf16[3,512,64]{2,1,0:T(8,128)(2,1)S(1)} %get-tuple-element.66.keys, bf16[3,512,64]{2,1,0:T(8,128)(2,1)S(1)} %get-tuple-element.67.values), custom_call_target="tpu_custom_call" | custom-call | flops 3300000000 | bytes 202752 | tf_op jit(solution)/shard_map/attend_0/pallas_call | solution.py:617
  65.1 2.7 %attend_2.1 = (bf16[512,192]{1,0:T(8,128)(2,1)S(1)}, f32[3,512,1]{2,1,0:T(8,128)S(1)}, f32[512,576]{1,0:T(8,128)S(1)}, bf16[512,576]{1,0:T(8,128)(2,1)S(1)}) custom-call(f32[512,512]{1,0:T(8,128)S(1)} %get-tuple-element.61.bias, bf16[9,512,64]{2,1,0:T(8,128)(2,1)S(1)} %get-tuple-element.65.query, bf16[3,512,64]{2,1,0:T(8,128)(2,1)S(1)} %get-tuple-element.66.keys, ...), custom_call_target="tpu_custom_call" | custom-call | flops 4400000000 | bytes 1972224 | tf_op jit(solution)/shard_map/attend_2/pallas_call | solution.py:617
  67.8 1.2 copy-done.9
  68.9 1.1 copy-done.19
  70.0 25.1 %feed.1 = (bf16[576,512]{1,0:T(8,128)(2,1)}, f32[512,576]{1,0:T(8,128)}, f32[8,576]{1,0:T(8,128)S(1)}, bf16[2,2,4,144,384]{4,3,2,1,0:T(8,128)(2,1)}, bf16[2,2,4,...) custom-call(s32[4]{0:T(128)S(1)} %pad_add_fusion.where_ref, ...), custom_call_target="tpu_custom_call" | custom-call | flops 20899999744 | bytes 7096320 | tf_op jit(solution)/shard_map/feed/pallas_call | solution.py:617
  95.1 1.3 copy-done.10
  96.4 0.9 copy-done.15
  97.4 2.9 %back_1.1 = (bf16[512,256]{1,0:T(8,128)(2,1)S(1)}, bf16[512,64]{1,0:T(8,128)(2,1)S(1)}, bf16[192,576]{1,0:T(8,128)(2,1)S(1)}) custom-call(f32[512,512]{1,0:T(8,128)S(1)} %get-tuple-element.61.bias, f32[512,128]{1,0:T(8,128)S(1)} %get-tuple-element.63.cosine, f32[512,128]{1,0:T(8,128)S(1)} %copy-done.15, bf16[640,1536]{1,0:T(8,128)(2,1)S(1)} %get-tuple-element.70.weights, ...), custom_call_target="tpu_custom_call" | custom-call | flops 5500000256 | bytes 548864 | tf_op jit(solution)/shard_map/back_1/pallas_call | solution.py:617
  100.3 2.9 %back_0.1 = (bf16[512,256]{1,0:T(8,128)(2,1)S(1)}, bf16[512,64]{1,0:T(8,128)(2,1)S(1)}, bf16[192,576]{1,0:T(8,128)(2,1)S(1)}) custom-call(f32[512,512]{1,0:T(8,128)S(1)} %get-tuple-element.61.bias, f32[512,128]{1,0:T(8,128)S(1)} %get-tuple-element.63.cosine, f32[512,128]{1,0:T(8,128)S(1)} %copy-done.15, bf16[640,1536]{1,0:T(8,128)(2,1)S(1)} %get-tuple-element.70.weights, ...), custom_call_target="tpu_custom_call" | custom-call | flops 5500000256 | bytes 548864 | tf_op jit(solution)/shard_map/back_0/pallas_call | solution.py:617
  103.8 2.9 %back_2.1 = (bf16[512,256]{1,0:T(8,128)(2,1)S(1)}, bf16[512,64]{1,0:T(8,128)(2,1)S(1)}, bf16[192,576]{1,0:T(8,128)(2,1)S(1)}) custom-call(f32[512,512]{1,0:T(8,128)S(1)} %get-tuple-element.61.bias, f32[512,128]{1,0:T(8,128)S(1)} %get-tuple-element.63.cosine, f32[512,128]{1,0:T(8,128)S(1)} %copy-done.15, bf16[640,1536]{1,0:T(8,128)(2,1)S(1)} %get-tuple-element.70.weights, ...), custom_call_target="tpu_custom_call" | custom-call | flops 5500000256 | bytes 548864 | tf_op jit(solution)/shard_map/back_2/pallas_call | solution.py:617
  106.7 5.1 %back_last.1 = (bf16[576,512]{1,0:T(8,128)(2,1)}, bf16[2,2,4,80,384]{4,3,2,1,0:T(8,128)(2,1)S(1)}, bf16[2,2,4,80,384]{4,3,2,1,0:T(8,128)(2,1)S(1)}) custom-call(s32[4]{0:T(128)S(1)} %pad_add_fusion.where_ref, f32[512,576]{1,0:T(8,128)S(1)} %get-tuple-element.68.hidden_in, f32[8,576]{1,0:T(8,128)S(1)} %get-tuple-element.69.gains, ...), custom_call_target="tpu_custom_call" | custom-call | flops 6600000000 | bytes 2555904 | tf_op jit(solution)/shard_map/back_last/pallas_call | solution.py:617
  113.2 1.4 collective-permute-done.18
  116.4 10.4 %collective-permute-done.37 = bf16[2,4,48,576]{3,2,1,0:T(8,128)(2,1)S(1)} collective-permute-done((bf16[2,4,48,576]{3,2,1,0:T(8,128)(2,1)S(1)}, bf16[2,4,48,576]{3,2,1,0:T(8,128)(2,1)S(1)}, u32[]{:S(2)}, u32[]{:S(2)}) %collective-permute-start.37) | collective-permute-done | bytes 442400 | tf_op jit(solution)/shard_map/ppermute | solution.py:46
  127.5 9.0 %collective-permute-done.19 = bf16[2,4,80,384]{3,2,1,0:T(8,128)(2,1)S(1)} collective-permute-done((bf16[2,4,80,384]{3,2,1,0:T(8,128)(2,1)S(1)}, bf16[2,4,80,384]{3,2,1,0:T(8,128)(2,1)S(1)}, u32[]{:S(2)}, u32[]{:S(2)}) %collective-permute-start.19) | collective-permute-done | bytes 491552 | tf_op jit(solution)/shard_map/ppermute | solution.py:46
  137.1 6.5 %collective-permute-done.38 = bf16[4,48,576]{2,1,0:T(8,128)(2,1)S(1)} collective-permute-done((bf16[4,48,576]{2,1,0:T(8,128)(2,1)S(1)}, bf16[4,48,576]{2,1,0:T(8,128)(2,1)S(1)}, u32[]{:S(2)}, u32[]{:S(2)}) %collective-permute-start.38) | collective-permute-done | bytes 221216 | tf_op jit(solution)/shard_map/ppermute | solution.py:46
  143.7 1.9 %collective-permute-start.39 = (bf16[48,576]{1,0:T(8,128)(2,1)S(1)}, bf16[48,576]{1,0:T(8,128)(2,1)S(1)}, u32[]{:S(2)}, u32[]{:S(2)}) collective-permute-start(bf16[48,576]{1,0:T(8,128)(2,1)S(1)} %get-tuple-element.128), channel_id=1, source_target_pairs={{0,1},{1,2},{2,3},{3,0},{4,5},{5,6},{6,7},{7,4},{8,9},{9,10},{10,1... | collective-permute-start | bytes 165896 | tf_op jit(solution)/shard_map/ppermute | solution.py:54
  145.6 2.0 %collective-permute-start.41 = (bf16[48,576]{1,0:T(8,128)(2,1)S(1)}, bf16[48,576]{1,0:T(8,128)(2,1)S(1)}, u32[]{:S(2)}, u32[]{:S(2)}) collective-permute-start(bf16[48,576]{1,0:T(8,128)(2,1)S(1)} %get-tuple-element.129), channel_id=1, source_target_pairs={{0,3},{1,0},{2,1},{3,2},{4,7},{5,4},{6,5},{7,6},{8,11},{9,8},{10,9... | collective-permute-start | bytes 165896 | tf_op jit(solution)/shard_map/ppermute | solution.py:54
  147.8 1.6 collective-permute-start.29
  149.9 1.2 collective-permute-done.41
  151.1 1.8 collective-permute-done.40
  152.9 1.0 collective-permute-start.42
  154.1 3.8 %collective-permute-start.23 = (bf16[80,384]{1,0:T(8,128)(2,1)S(1)}, bf16[80,384]{1,0:T(8,128)(2,1)S(1)}, u32[]{:S(2)}, u32[]{:S(2)}) collective-permute-start(bf16[80,384]{1,0:T(8,128)(2,1)S(1)} %get-tuple-element.132), channel_id=1, source_target_pairs={{0,3},{1,0},{2,1},{3,2},{4,7},{5,4},{6,5},{7,6},{8,11},{9,8},{10,9... | collective-permute-start | bytes 184328 | tf_op jit(solution)/shard_map/ppermute | solution.py:54
  158.0 1.3 collective-permute-start.30
  159.3 1.4 collective-permute-done.21
  160.7 1.1 collective-permute-start.32
  161.9 1.1 collective-permute-start.31
  163.0 3.7 %collective-permute-done.22 = bf16[80,384]{1,0:T(8,128)(2,1)S(1)} collective-permute-done((bf16[80,384]{1,0:T(8,128)(2,1)S(1)}, bf16[80,384]{1,0:T(8,128)(2,1)S(1)}, u32[]{:S(2)}, u32[]{:S(2)}) %collective-permute-start.22) | collective-permute-done | bytes 61472 | tf_op jit(solution)/shard_map/ppermute | solution.py:54
  166.7 1.1 collective-permute-start.24
  167.8 3.0 %collective-permute-done.31 = bf16[144,384]{1,0:T(8,128)(2,1)S(1)} collective-permute-done((bf16[144,384]{1,0:T(8,128)(2,1)S(1)}, bf16[144,384]{1,0:T(8,128)(2,1)S(1)}, u32[]{:S(2)}, u32[]{:S(2)}) %collective-permute-start.31) | collective-permute-done | bytes 110624 | tf_op jit(solution)/shard_map/ppermute | solution.py:54
  171.0 1.6 collective-permute-start.33
  173.1 2.6 %collective-permute-done.33 = bf16[144,384]{1,0:T(8,128)(2,1)S(1)} collective-permute-done((bf16[144,384]{1,0:T(8,128)(2,1)S(1)}, bf16[144,384]{1,0:T(8,128)(2,1)S(1)}, u32[]{:S(2)}, u32[]{:S(2)}) %collective-permute-start.33) | collective-permute-done | bytes 110624 | tf_op jit(solution)/shard_map/ppermute | solution.py:46
  175.8 1.3 collective-permute-start.34
  177.2 1.5 collective-permute-start.43
  178.8 3.0 %collective-permute-done.34 = bf16[2,144,384]{2,1,0:T(8,128)(2,1)S(1)} collective-permute-done((bf16[2,144,384]{2,1,0:T(8,128)(2,1)S(1)}, bf16[2,144,384]{2,1,0:T(8,128)(2,1)S(1)}, u32[]{:S(2)}, u32[]{:S(2)}) %collective-permute-start.34) | collective-permute-done | bytes 221216 | tf_op jit(solution)/shard_map/ppermute | solution.py:46
  182.6 1.7 finish_attn.1
  184.3 0.6 fusion.54
  184.9 3.2 %finish_feed.1 = (f32[144,1536]{1,0:T(8,128)}, f32[144,1536]{1,0:T(8,128)}, f32[576,384]{1,0:T(8,128)}) custom-call(s32[4]{0:T(128)S(1)} %pad_add_fusion.where_ref, bf16[2,2,144,384]{3,2,1,0:T(8,128)(2,1)S(1)} %pad_maximum_fusion.4.pair_pieces, bf16[2,2,144,384]{3,2,1,0:T(8,128)(2,1)S(1)} %collective-permute-done.35.pair_other, ...), custom_call_target="tpu_custom_call" | custom-call | flops 3300000000 | bytes 2654208 | tf_op jit(solution)/shard_map/finish_feed/pallas_call | solution.py:617
  (117 shorter events, 11.5 us)
Async XLA Ops:
  0.6 10.5 %copy-start.3 = (bf16[144,1536]{1,0:T(8,128)(2,1)S(1)}, bf16[144,1536]{1,0:T(8,128)(2,1)}, u32[]{:S(2)}) copy-start(bf16[144,1536]{1,0:T(8,128)(2,1)} %own_gate.1) | copy-start | bytes 1327108
  0.7 10.5 %copy-start.6 = (s32[1,4]{1,0:T(1,128)S(1)}, s32[1,4]{1,0:T(1,128)}, u32[]{:S(2)}) copy-start(s32[1,4]{1,0:T(1,128)} %lengths.3) | copy-start | bytes 52
  0.7 10.5 %copy-start.1 = (bf16[512,576]{0,1:T(8,128)(2,1)S(1)}, bf16[512,576]{0,1:T(8,128)(2,1)}, u32[]{:S(2)}) copy-start(bf16[512,576]{0,1:T(8,128)(2,1)} %param.25) | copy-start | bytes 1769476
  0.7 10.5 %copy-start.2 = (bf16[384,576]{0,1:T(8,128)(2,1)S(1)}, bf16[384,576]{0,1:T(8,128)(2,1)}, u32[]{:S(2)}) copy-start(bf16[384,576]{0,1:T(8,128)(2,1)} %param.24) | copy-start | bytes 1327108
  0.7 10.5 %copy-start = (bf16[512,576]{0,1:T(8,128)(2,1)S(1)}, bf16[512,576]{0,1:T(8,128)(2,1)}, u32[]{:S(2)}) copy-start(bf16[512,576]{0,1:T(8,128)(2,1)} %param.14) | copy-start | bytes 1769476
  3.9 12.9 %collective-permute-start.2 = (bf16[80,384]{1,0:T(8,128)(2,1)S(1)}, bf16[80,384]{1,0:T(8,128)(2,1)S(1)}, u32[]{:S(2)}, u32[]{:S(2)}) collective-permute-start(bf16[80,384]{1,0:T(8,128)(2,1)S(1)} %dynamic_slice.6), channel_id=1, source_target_pairs={{3,0},{0,1},{1,2},{2,3},{7,4},{4,5},{5,6},{6,7},{11,8},{8,9},{9,10... | collective-permute-start | bytes 184328 | tf_op jit(solution)/shard_map/ppermute | solution.py:50
  7.1 12.6 %collective-permute-start.1 = (bf16[80,384]{1,0:T(8,128)(2,1)S(1)}, bf16[80,384]{1,0:T(8,128)(2,1)S(1)}, u32[]{:S(2)}, u32[]{:S(2)}) collective-permute-start(bf16[80,384]{1,0:T(8,128)(2,1)S(1)} %dynamic_slice.6), channel_id=1, source_target_pairs={{2,0},{3,1},{0,2},{1,3},{6,4},{7,5},{4,6},{5,7},{10,8},{11,9},{8,1... | collective-permute-start | bytes 184328 | tf_op jit(solution)/shard_map/ppermute | solution.py:50
  9.7 10.0 %collective-permute-start = (bf16[80,384]{1,0:T(8,128)(2,1)S(1)}, bf16[80,384]{1,0:T(8,128)(2,1)S(1)}, u32[]{:S(2)}, u32[]{:S(2)}) collective-permute-start(bf16[80,384]{1,0:T(8,128)(2,1)S(1)} %dynamic_slice.6), channel_id=1, source_target_pairs={{1,0},{2,1},{3,2},{0,3},{5,4},{6,5},{7,6},{4,7},{9,8},{10,9},{11,1... | collective-permute-start | bytes 184328 | tf_op jit(solution)/shard_map/ppermute | solution.py:50
  11.2 1.0 copy-start.4
  12.2 1.0 copy-start.7
  13.1 1.0 copy-start.8
  15.8 41.6 %copy-start.14 = (f32[512,128]{1,0:T(8,128)}, f32[512,128]{1,0:T(8,128)S(1)}, u32[]{:S(2)}) copy-start(f32[512,128]{1,0:T(8,128)S(1)} %get-tuple-element.64.sine) | copy-start | bytes 786436
  15.8 7.9 %collective-permute-start.8 = (bf16[144,384]{1,0:T(8,128)(2,1)S(1)}, bf16[144,384]{1,0:T(8,128)(2,1)S(1)}, u32[]{:S(2)}, u32[]{:S(2)}) collective-permute-start(bf16[144,384]{1,0:T(8,128)(2,1)S(1)} %get-tuple-element.77), channel_id=1, source_target_pairs={{3,0},{0,1},{1,2},{2,3},{7,4},{4,5},{5,6},{6,7},{11,8},{8,9},{9,10... | collective-permute-start | bytes 331784 | tf_op jit(solution)/shard_map/ppermute | solution.py:50
  16.5 10.0 %collective-permute-start.7 = (bf16[144,384]{1,0:T(8,128)(2,1)S(1)}, bf16[144,384]{1,0:T(8,128)(2,1)S(1)}, u32[]{:S(2)}, u32[]{:S(2)}) collective-permute-start(bf16[144,384]{1,0:T(8,128)(2,1)S(1)} %get-tuple-element.77), channel_id=1, source_target_pairs={{2,0},{3,1},{0,2},{1,3},{6,4},{7,5},{4,6},{5,7},{10,8},{11,9},{8,1... | collective-permute-start | bytes 331784 | tf_op jit(solution)/shard_map/ppermute | solution.py:50
  16.9 9.7 %collective-permute-start.6 = (bf16[144,384]{1,0:T(8,128)(2,1)S(1)}, bf16[144,384]{1,0:T(8,128)(2,1)S(1)}, u32[]{:S(2)}, u32[]{:S(2)}) collective-permute-start(bf16[144,384]{1,0:T(8,128)(2,1)S(1)} %get-tuple-element.77), channel_id=1, source_target_pairs={{1,0},{2,1},{3,2},{0,3},{5,4},{6,5},{7,6},{4,7},{9,8},{10,9},{11,1... | collective-permute-start | bytes 331784 | tf_op jit(solution)/shard_map/ppermute | solution.py:50
  19.7 8.5 %collective-permute-start.3 = (bf16[3,80,384]{2,1,0:T(8,128)(2,1)S(1)}, bf16[3,80,384]{2,1,0:T(8,128)(2,1)S(1)}, u32[]{:S(2)}, u32[]{:S(2)}) collective-permute-start(bf16[3,80,384]{2,1,0:T(8,128)(2,1)S(1)} %get-tuple-element.145), channel_id=1, source_target_pairs={{0,16},{4,20},{8,24},{12,28},{16,0},{20,4},{24,8},{28,12},{1,17},{... | collective-permute-start | bytes 552968 | tf_op jit(solution)/shard_map/ppermute | solution.py:46
  26.6 12.1 %collective-permute-start.9 = (bf16[3,144,384]{2,1,0:T(8,128)(2,1)S(1)}, bf16[3,144,384]{2,1,0:T(8,128)(2,1)S(1)}, u32[]{:S(2)}, u32[]{:S(2)}) collective-permute-start(bf16[3,144,384]{2,1,0:T(8,128)(2,1)S(1)} %get-tuple-element.139), channel_id=1, source_target_pairs={{0,16},{4,20},{8,24},{12,28},{16,0},{20,4},{24,8},{28,12},{1,17},{... | collective-permute-start | bytes 995336 | tf_op jit(solution)/shard_map/ppermute | solution.py:46
  28.3 12.1 %collective-permute-start.4 = (bf16[2,3,80,384]{3,2,1,0:T(8,128)(2,1)S(1)}, bf16[2,3,80,384]{3,2,1,0:T(8,128)(2,1)S(1)}, u32[]{:S(2)}, u32[]{:S(2)}) collective-permute-start(bf16[2,3,80,384]{3,2,1,0:T(8,128)(2,1)S(1)} %get-tuple-element.137), channel_id=1, source_target_pairs={{0,8},{4,12},{8,0},{12,4},{16,24},{20,28},{24,16},{28,20},{1,9},{5... | collective-permute-start | bytes 1105928 | tf_op jit(solution)/shard_map/ppermute | solution.py:46
  29.9 6.2 %collective-permute-start.14 = (bf16[48,576]{1,0:T(8,128)(2,1)S(1)}, bf16[48,576]{1,0:T(8,128)(2,1)S(1)}, u32[]{:S(2)}, u32[]{:S(2)}) collective-permute-start(bf16[48,576]{1,0:T(8,128)(2,1)S(1)} %get-tuple-element.78), channel_id=1, source_target_pairs={{3,0},{0,1},{1,2},{2,3},{7,4},{4,5},{5,6},{6,7},{11,8},{8,9},{9,10... | collective-permute-start | bytes 165896 | tf_op jit(solution)/shard_map/ppermute | solution.py:50
  32.1 5.9 %collective-permute-start.13 = (bf16[48,576]{1,0:T(8,128)(2,1)S(1)}, bf16[48,576]{1,0:T(8,128)(2,1)S(1)}, u32[]{:S(2)}, u32[]{:S(2)}) collective-permute-start(bf16[48,576]{1,0:T(8,128)(2,1)S(1)} %get-tuple-element.78), channel_id=1, source_target_pairs={{2,0},{3,1},{0,2},{1,3},{6,4},{7,5},{4,6},{5,7},{10,8},{11,9},{8,1... | collective-permute-start | bytes 165896 | tf_op jit(solution)/shard_map/ppermute | solution.py:50
  32.7 5.4 %collective-permute-start.12 = (bf16[48,576]{1,0:T(8,128)(2,1)S(1)}, bf16[48,576]{1,0:T(8,128)(2,1)S(1)}, u32[]{:S(2)}, u32[]{:S(2)}) collective-permute-start(bf16[48,576]{1,0:T(8,128)(2,1)S(1)} %get-tuple-element.78), channel_id=1, source_target_pairs={{1,0},{2,1},{3,2},{0,3},{5,4},{6,5},{7,6},{4,7},{9,8},{10,9},{11,1... | collective-permute-start | bytes 165896 | tf_op jit(solution)/shard_map/ppermute | solution.py:50
  38.1 7.6 %collective-permute-start.15 = (bf16[3,48,576]{2,1,0:T(8,128)(2,1)S(1)}, bf16[3,48,576]{2,1,0:T(8,128)(2,1)S(1)}, u32[]{:S(2)}, u32[]{:S(2)}) collective-permute-start(bf16[3,48,576]{2,1,0:T(8,128)(2,1)S(1)} %get-tuple-element.143), channel_id=1, source_target_pairs={{0,8},{4,12},{8,0},{12,4},{16,24},{20,28},{24,16},{28,20},{1,9},{5... | collective-permute-start | bytes 497672 | tf_op jit(solution)/shard_map/ppermute | solution.py:46
  38.8 18.3 %collective-permute-start.10 = (bf16[2,3,144,384]{3,2,1,0:T(8,128)(2,1)S(1)}, bf16[2,3,144,384]{3,2,1,0:T(8,128)(2,1)S(1)}, u32[]{:S(2)}, u32[]{:S(2)}) collective-permute-start(bf16[2,3,144,384]{3,2,1,0:T(8,128)(2,1)S(1)} %get-tuple-element.127), channel_id=1, source_target_pairs={{0,8},{4,12},{8,0},{12,4},{16,24},{20,28},{24,16},{28,20},{1,9},{5... | collective-permute-start | bytes 1990664 | tf_op jit(solution)/shard_map/ppermute | solution.py:46
  40.5 16.9 %collective-permute-start.5 = (bf16[2,2,3,80,384]{4,3,2,1,0:T(8,128)(2,1)S(1)}, bf16[2,2,3,80,384]{4,3,2,1,0:T(8,128)(2,1)S(1)}, u32[]{:S(2)}, u32[]{:S(2)}) collective-permute-start(bf16[2,2,3,80,384]{4,3,2,1,0:T(8,128)(2,1)S(1)} %pad_maximum_fusion.1.pieces), channel_id=1, source_target_pairs={{0,4},{4,0},{8,12},{12,8},{16,20},{20,16},{24,28},{28,24},{1,5},{5... | collective-permute-start | bytes 2211848 | tf_op jit(solution)/shard_map/ppermute | solution.py:46
  45.8 7.6 %collective-permute-start.16 = (bf16[2,3,48,576]{3,2,1,0:T(8,128)(2,1)S(1)}, bf16[2,3,48,576]{3,2,1,0:T(8,128)(2,1)S(1)}, u32[]{:S(2)}, u32[]{:S(2)}) collective-permute-start(bf16[2,3,48,576]{3,2,1,0:T(8,128)(2,1)S(1)} %get-tuple-element.135), channel_id=1, source_target_pairs={{0,16},{4,20},{8,24},{12,28},{16,0},{20,4},{24,8},{28,12},{1,17},{... | collective-permute-start | bytes 995336 | tf_op jit(solution)/shard_map/ppermute | solution.py:46
  53.5 15.4 %collective-permute-start.17 = (bf16[2,2,3,48,576]{4,3,2,1,0:T(8,128)(2,1)S(1)}, bf16[2,2,3,48,576]{4,3,2,1,0:T(8,128)(2,1)S(1)}, u32[]{:S(2)}, u32[]{:S(2)}) collective-permute-start(bf16[2,2,3,48,576]{4,3,2,1,0:T(8,128)(2,1)S(1)} %pad_maximum_fusion.2.down_pieces), channel_id=1, source_target_pairs={{0,4},{4,0},{8,12},{12,8},{16,20},{20,16},{24,28},{28,24},{1,5},{5... | collective-permute-start | bytes 1990664 | tf_op jit(solution)/shard_map/ppermute | solution.py:46
  57.3 4.0 %copy-start.17 = (bf16[2,2,3,144,384]{4,3,2,1,0:T(8,128)(2,1)}, bf16[2,2,3,144,384]{4,3,2,1,0:T(8,128)(2,1)S(1)}, u32[]{:S(2)}) copy-start(bf16[2,2,3,144,384]{4,3,2,1,0:T(8,128)(2,1)S(1)} %pad_maximum_fusion.pair_pieces) | copy-start | bytes 3981316
  57.3 11.7 %collective-permute-start.11 = (bf16[2,2,3,144,384]{4,3,2,1,0:T(8,128)(2,1)S(1)}, bf16[2,2,3,144,384]{4,3,2,1,0:T(8,128)(2,1)S(1)}, u32[]{:S(2)}, u32[]{:S(2)}) collective-permute-start(bf16[2,2,3,144,384]{4,3,2,1,0:T(8,128)(2,1)S(1)} %pad_maximum_fusion.pair_pieces), channel_id=1, source_target_pairs={{0,4},{4,0},{8,12},{12,8},{16,20},{20,16},{24,28},{28,24},{1,5},{5... | collective-permute-start | bytes 3981320 | tf_op jit(solution)/shard_map/ppermute | solution.py:46
  61.2 1.9 %copy-start.12 = (bf16[512,576]{1,0:T(8,128)(2,1)}, bf16[512,576]{1,0:T(8,128)(2,1)S(1)}, u32[]{:S(2)}) copy-start(bf16[512,576]{1,0:T(8,128)(2,1)S(1)} %get-tuple-element.80.normed) | copy-start | bytes 1769476
  65.1 4.9 %copy-start.5 = (bf16[144,1536]{1,0:T(8,128)(2,1)S(1)}, bf16[144,1536]{1,0:T(8,128)(2,1)}, u32[]{:S(2)}) copy-start(bf16[144,1536]{1,0:T(8,128)(2,1)} %own_up.1) | copy-start | bytes 1327108
  67.8 1.2 copy-start.9
  68.9 1.1 copy-start.19
  95.1 1.3 copy-start.10
  100.3 3.5 %copy-start.18 = (bf16[2,2,4,144,384]{4,3,2,1,0:T(8,128)(2,1)S(1)}, bf16[2,2,4,144,384]{4,3,2,1,0:T(8,128)(2,1)}, u32[]{:S(2)}) copy-start(bf16[2,2,4,144,384]{4,3,2,1,0:T(8,128)(2,1)} %get-tuple-element.105) | copy-start | bytes 5308420
  103.2 9.2 %collective-permute-start.36 = (bf16[2,2,4,48,576]{4,3,2,1,0:T(8,128)(2,1)S(1)}, bf16[2,2,4,48,576]{4,3,2,1,0:T(8,128)(2,1)S(1)}, u32[]{:S(2)}, u32[]{:S(2)}) collective-permute-start(bf16[2,2,4,48,576]{4,3,2,1,0:T(8,128)(2,1)S(1)} %get-tuple-element.107), channel_id=1, source_target_pairs={{0,4},{4,0},{8,12},{12,8},{16,20},{20,16},{24,28},{28,24},{1,5},{5... | collective-permute-start | bytes 2654216 | tf_op jit(solution)/shard_map/ppermute | solution.py:46
  103.7 11.7 %collective-permute-start.27 = (bf16[2,2,4,144,384]{4,3,2,1,0:T(8,128)(2,1)S(1)}, bf16[2,2,4,144,384]{4,3,2,1,0:T(8,128)(2,1)S(1)}, u32[]{:S(2)}, u32[]{:S(2)}) collective-permute-start(bf16[2,2,4,144,384]{4,3,2,1,0:T(8,128)(2,1)S(1)} %copy-done.18), channel_id=1, source_target_pairs={{0,4},{4,0},{8,12},{12,8},{16,20},{20,16},{24,28},{28,24},{1,5},{5... | collective-permute-start | bytes 5308424 | tf_op jit(solution)/shard_map/ppermute | solution.py:46
  103.8 2.9 %copy-start.11 = (f32[512,576]{1,0:T(8,128)S(1)}, f32[512,576]{1,0:T(8,128)}, u32[]{:S(2)}) copy-start(f32[512,576]{1,0:T(8,128)} %get-tuple-element.81.grad_one) | copy-start | bytes 3538948
  103.8 2.9 %copy-start.13 = (bf16[512,576]{1,0:T(8,128)(2,1)S(1)}, bf16[512,576]{1,0:T(8,128)(2,1)}, u32[]{:S(2)}) copy-start(bf16[512,576]{1,0:T(8,128)(2,1)} %copy-done.12) | copy-start | bytes 1769476
  111.9 2.7 %collective-permute-start.18 = (bf16[2,2,4,80,384]{4,3,2,1,0:T(8,128)(2,1)S(1)}, bf16[2,2,4,80,384]{4,3,2,1,0:T(8,128)(2,1)S(1)}, u32[]{:S(2)}, u32[]{:S(2)}) collective-permute-start(bf16[2,2,4,80,384]{4,3,2,1,0:T(8,128)(2,1)S(1)} %get-tuple-element.98), channel_id=1, source_target_pairs={{0,4},{4,0},{8,12},{12,8},{16,20},{20,16},{24,28},{28,24},{1,5},{5... | collective-permute-start | bytes 2949128 | tf_op jit(solution)/shard_map/ppermute | solution.py:46
  112.6 2.8 %copy-start.16 = (bf16[2,2,4,144,384]{4,3,2,1,0:T(8,128)(2,1)S(1)}, bf16[2,2,4,144,384]{4,3,2,1,0:T(8,128)(2,1)}, u32[]{:S(2)}) copy-start(bf16[2,2,4,144,384]{4,3,2,1,0:T(8,128)(2,1)} %get-tuple-element.104) | copy-start | bytes 5308420
  112.6 14.1 %collective-permute-start.37 = (bf16[2,4,48,576]{3,2,1,0:T(8,128)(2,1)S(1)}, bf16[2,4,48,576]{3,2,1,0:T(8,128)(2,1)S(1)}, u32[]{:S(2)}, u32[]{:S(2)}) collective-permute-start(bf16[2,4,48,576]{3,2,1,0:T(8,128)(2,1)S(1)} %get-tuple-element.114), channel_id=1, source_target_pairs={{0,16},{4,20},{8,24},{12,28},{16,0},{20,4},{24,8},{28,12},{1,17},{... | collective-permute-start | bytes 1327112 | tf_op jit(solution)/shard_map/ppermute | solution.py:46
  114.8 21.6 %collective-permute-start.19 = (bf16[2,4,80,384]{3,2,1,0:T(8,128)(2,1)S(1)}, bf16[2,4,80,384]{3,2,1,0:T(8,128)(2,1)S(1)}, u32[]{:S(2)}, u32[]{:S(2)}) collective-permute-start(bf16[2,4,80,384]{3,2,1,0:T(8,128)(2,1)S(1)} %get-tuple-element.116), channel_id=1, source_target_pairs={{0,16},{4,20},{8,24},{12,28},{16,0},{20,4},{24,8},{28,12},{1,17},{... | collective-permute-start | bytes 1474568 | tf_op jit(solution)/shard_map/ppermute | solution.py:46
  115.8 31.8 %collective-permute-start.28 = (bf16[2,4,144,384]{3,2,1,0:T(8,128)(2,1)S(1)}, bf16[2,4,144,384]{3,2,1,0:T(8,128)(2,1)S(1)}, u32[]{:S(2)}, u32[]{:S(2)}) collective-permute-start(bf16[2,4,144,384]{3,2,1,0:T(8,128)(2,1)S(1)} %get-tuple-element.112), channel_id=1, source_target_pairs={{0,8},{4,12},{8,0},{12,4},{16,24},{20,28},{24,16},{28,20},{1,9},{5... | collective-permute-start | bytes 2654216 | tf_op jit(solution)/shard_map/ppermute | solution.py:46
  126.9 16.8 %collective-permute-start.38 = (bf16[4,48,576]{2,1,0:T(8,128)(2,1)S(1)}, bf16[4,48,576]{2,1,0:T(8,128)(2,1)S(1)}, u32[]{:S(2)}, u32[]{:S(2)}) collective-permute-start(bf16[4,48,576]{2,1,0:T(8,128)(2,1)S(1)} %get-tuple-element.120), channel_id=1, source_target_pairs={{0,8},{4,12},{8,0},{12,4},{16,24},{20,28},{24,16},{28,20},{1,9},{5... | collective-permute-start | bytes 663560 | tf_op jit(solution)/shard_map/ppermute | solution.py:46
  136.6 17.4 %collective-permute-start.20 = (bf16[4,80,384]{2,1,0:T(8,128)(2,1)S(1)}, bf16[4,80,384]{2,1,0:T(8,128)(2,1)S(1)}, u32[]{:S(2)}, u32[]{:S(2)}) collective-permute-start(bf16[4,80,384]{2,1,0:T(8,128)(2,1)S(1)} %get-tuple-element.122), channel_id=1, source_target_pairs={{0,8},{4,12},{8,0},{12,4},{16,24},{20,28},{24,16},{28,20},{1,9},{5... | collective-permute-start | bytes 737288 | tf_op jit(solution)/shard_map/ppermute | solution.py:46
  143.7 6.2 %collective-permute-start.39 = (bf16[48,576]{1,0:T(8,128)(2,1)S(1)}, bf16[48,576]{1,0:T(8,128)(2,1)S(1)}, u32[]{:S(2)}, u32[]{:S(2)}) collective-permute-start(bf16[48,576]{1,0:T(8,128)(2,1)S(1)} %get-tuple-element.128), channel_id=1, source_target_pairs={{0,1},{1,2},{2,3},{3,0},{4,5},{5,6},{6,7},{7,4},{8,9},{9,10},{10,1... | collective-permute-start | bytes 165896 | tf_op jit(solution)/shard_map/ppermute | solution.py:54
  145.6 5.4 %collective-permute-start.41 = (bf16[48,576]{1,0:T(8,128)(2,1)S(1)}, bf16[48,576]{1,0:T(8,128)(2,1)S(1)}, u32[]{:S(2)}, u32[]{:S(2)}) collective-permute-start(bf16[48,576]{1,0:T(8,128)(2,1)S(1)} %get-tuple-element.129), channel_id=1, source_target_pairs={{0,3},{1,0},{2,1},{3,2},{4,7},{5,4},{6,5},{7,6},{8,11},{9,8},{10,9... | collective-permute-start | bytes 165896 | tf_op jit(solution)/shard_map/ppermute | solution.py:54
  147.6 5.3 %collective-permute-start.40 = (bf16[48,576]{1,0:T(8,128)(2,1)S(1)}, bf16[48,576]{1,0:T(8,128)(2,1)S(1)}, u32[]{:S(2)}, u32[]{:S(2)}) collective-permute-start(bf16[48,576]{1,0:T(8,128)(2,1)S(1)} %get-tuple-element.130), channel_id=1, source_target_pairs={{0,2},{1,3},{2,0},{3,1},{4,6},{5,7},{6,4},{7,5},{8,10},{9,11},{10,... | collective-permute-start | bytes 165896 | tf_op jit(solution)/shard_map/ppermute | solution.py:54
  147.8 10.1 %collective-permute-start.29 = (bf16[4,144,384]{2,1,0:T(8,128)(2,1)S(1)}, bf16[4,144,384]{2,1,0:T(8,128)(2,1)S(1)}, u32[]{:S(2)}, u32[]{:S(2)}) collective-permute-start(bf16[4,144,384]{2,1,0:T(8,128)(2,1)S(1)} %get-tuple-element.118), channel_id=1, source_target_pairs={{0,16},{4,20},{8,24},{12,28},{16,0},{20,4},{24,8},{28,12},{1,17},{... | collective-permute-start | bytes 1327112 | tf_op jit(solution)/shard_map/ppermute | solution.py:46
  152.9 24.3 %collective-permute-start.42 = (bf16[48,576]{1,0:T(8,128)(2,1)S(1)}, bf16[48,576]{1,0:T(8,128)(2,1)S(1)}, u32[]{:S(2)}, u32[]{:S(2)}) collective-permute-start(bf16[48,576]{1,0:T(8,128)(2,1)S(1)} %fusion.27), channel_id=1, source_target_pairs={{0,8},{4,12},{8,0},{12,4},{16,24},{20,28},{24,16},{28,20},{1,9},{5... | collective-permute-start | bytes 165896 | tf_op jit(solution)/shard_map/ppermute | solution.py:46
  154.0 6.7 %collective-permute-start.21 = (bf16[80,384]{1,0:T(8,128)(2,1)S(1)}, bf16[80,384]{1,0:T(8,128)(2,1)S(1)}, u32[]{:S(2)}, u32[]{:S(2)}) collective-permute-start(bf16[80,384]{1,0:T(8,128)(2,1)S(1)} %get-tuple-element.131), channel_id=1, source_target_pairs={{0,1},{1,2},{2,3},{3,0},{4,5},{5,6},{6,7},{7,4},{8,9},{9,10},{10,1... | collective-permute-start | bytes 184328 | tf_op jit(solution)/shard_map/ppermute | solution.py:54
  154.1 7.8 %collective-permute-start.23 = (bf16[80,384]{1,0:T(8,128)(2,1)S(1)}, bf16[80,384]{1,0:T(8,128)(2,1)S(1)}, u32[]{:S(2)}, u32[]{:S(2)}) collective-permute-start(bf16[80,384]{1,0:T(8,128)(2,1)S(1)} %get-tuple-element.132), channel_id=1, source_target_pairs={{0,3},{1,0},{2,1},{3,2},{4,7},{5,4},{6,5},{7,6},{8,11},{9,8},{10,9... | collective-permute-start | bytes 184328 | tf_op jit(solution)/shard_map/ppermute | solution.py:54
  157.9 8.8 %collective-permute-start.22 = (bf16[80,384]{1,0:T(8,128)(2,1)S(1)}, bf16[80,384]{1,0:T(8,128)(2,1)S(1)}, u32[]{:S(2)}, u32[]{:S(2)}) collective-permute-start(bf16[80,384]{1,0:T(8,128)(2,1)S(1)} %get-tuple-element.133), channel_id=1, source_target_pairs={{0,2},{1,3},{2,0},{3,1},{4,6},{5,7},{6,4},{7,5},{8,10},{9,11},{10,... | collective-permute-start | bytes 184328 | tf_op jit(solution)/shard_map/ppermute | solution.py:54
  158.0 9.8 %collective-permute-start.30 = (bf16[144,384]{1,0:T(8,128)(2,1)S(1)}, bf16[144,384]{1,0:T(8,128)(2,1)S(1)}, u32[]{:S(2)}, u32[]{:S(2)}) collective-permute-start(bf16[144,384]{1,0:T(8,128)(2,1)S(1)} %get-tuple-element.123), channel_id=1, source_target_pairs={{0,1},{1,2},{2,3},{3,0},{4,5},{5,6},{6,7},{7,4},{8,9},{9,10},{10,1... | collective-permute-start | bytes 331784 | tf_op jit(solution)/shard_map/ppermute | solution.py:54
  160.7 7.1 %collective-permute-start.32 = (bf16[144,384]{1,0:T(8,128)(2,1)S(1)}, bf16[144,384]{1,0:T(8,128)(2,1)S(1)}, u32[]{:S(2)}, u32[]{:S(2)}) collective-permute-start(bf16[144,384]{1,0:T(8,128)(2,1)S(1)} %get-tuple-element.124), channel_id=1, source_target_pairs={{0,3},{1,0},{2,1},{3,2},{4,7},{5,4},{6,5},{7,6},{8,11},{9,8},{10,9... | collective-permute-start | bytes 331784 | tf_op jit(solution)/shard_map/ppermute | solution.py:54
  161.9 9.0 %collective-permute-start.31 = (bf16[144,384]{1,0:T(8,128)(2,1)S(1)}, bf16[144,384]{1,0:T(8,128)(2,1)S(1)}, u32[]{:S(2)}, u32[]{:S(2)}) collective-permute-start(bf16[144,384]{1,0:T(8,128)(2,1)S(1)} %get-tuple-element.125), channel_id=1, source_target_pairs={{0,2},{1,3},{2,0},{3,1},{4,6},{5,7},{6,4},{7,5},{8,10},{9,11},{10,... | collective-permute-start | bytes 331784 | tf_op jit(solution)/shard_map/ppermute | solution.py:54
  166.7 5.8 %collective-permute-start.24 = (bf16[80,384]{1,0:T(8,128)(2,1)S(1)}, bf16[80,384]{1,0:T(8,128)(2,1)S(1)}, u32[]{:S(2)}, u32[]{:S(2)}) collective-permute-start(bf16[80,384]{1,0:T(8,128)(2,1)S(1)} %fusion.35), channel_id=1, source_target_pairs={{0,8},{4,12},{8,0},{12,4},{16,24},{20,28},{24,16},{28,20},{1,9},{5... | collective-permute-start | bytes 184328 | tf_op jit(solution)/shard_map/ppermute | solution.py:46
  171.0 4.8 %collective-permute-start.33 = (bf16[144,384]{1,0:T(8,128)(2,1)S(1)}, bf16[144,384]{1,0:T(8,128)(2,1)S(1)}, u32[]{:S(2)}, u32[]{:S(2)}) collective-permute-start(bf16[144,384]{1,0:T(8,128)(2,1)S(1)} %fusion.19), channel_id=1, source_target_pairs={{0,16},{4,20},{8,24},{12,28},{16,0},{20,4},{24,8},{28,12},{1,17},{... | collective-permute-start | bytes 331784 | tf_op jit(solution)/shard_map/ppermute | solution.py:46
  172.6 6.1 %collective-permute-start.25 = (bf16[2,80,384]{2,1,0:T(8,128)(2,1)S(1)}, bf16[2,80,384]{2,1,0:T(8,128)(2,1)S(1)}, u32[]{:S(2)}, u32[]{:S(2)}) collective-permute-start(bf16[2,80,384]{2,1,0:T(8,128)(2,1)S(1)} %get-tuple-element.149), channel_id=1, source_target_pairs={{0,16},{4,20},{8,24},{12,28},{16,0},{20,4},{24,8},{28,12},{1,17},{... | collective-permute-start | bytes 368648 | tf_op jit(solution)/shard_map/ppermute | solution.py:46
  175.8 6.0 %collective-permute-start.34 = (bf16[2,144,384]{2,1,0:T(8,128)(2,1)S(1)}, bf16[2,144,384]{2,1,0:T(8,128)(2,1)S(1)}, u32[]{:S(2)}, u32[]{:S(2)}) collective-permute-start(bf16[2,144,384]{2,1,0:T(8,128)(2,1)S(1)} %get-tuple-element.141), channel_id=1, source_target_pairs={{0,8},{4,12},{8,0},{12,4},{16,24},{20,28},{24,16},{28,20},{1,9},{5... | collective-permute-start | bytes 663560 | tf_op jit(solution)/shard_map/ppermute | solution.py:46
  177.2 4.9 %collective-permute-start.43 = (bf16[2,48,576]{2,1,0:T(8,128)(2,1)S(1)}, bf16[2,48,576]{2,1,0:T(8,128)(2,1)S(1)}, u32[]{:S(2)}, u32[]{:S(2)}) collective-permute-start(bf16[2,48,576]{2,1,0:T(8,128)(2,1)S(1)} %get-tuple-element.147), channel_id=1, source_target_pairs={{0,16},{4,20},{8,24},{12,28},{16,0},{20,4},{24,8},{28,12},{1,17},{... | collective-permute-start | bytes 331784 | tf_op jit(solution)/shard_map/ppermute | solution.py:46
  178.8 3.8 %collective-permute-start.26 = (bf16[2,2,80,384]{3,2,1,0:T(8,128)(2,1)S(1)}, bf16[2,2,80,384]{3,2,1,0:T(8,128)(2,1)S(1)}, u32[]{:S(2)}, u32[]{:S(2)}) collective-permute-start(bf16[2,2,80,384]{3,2,1,0:T(8,128)(2,1)S(1)} %pad_maximum_fusion.8.pieces), channel_id=1, source_target_pairs={{0,4},{4,0},{8,12},{12,8},{16,20},{20,16},{24,28},{28,24},{1,5},{5... | collective-permute-start | bytes 737288 | tf_op jit(solution)/shard_map/ppermute | solution.py:46
  181.9 3.1 %collective-permute-start.35 = (bf16[2,2,144,384]{3,2,1,0:T(8,128)(2,1)S(1)}, bf16[2,2,144,384]{3,2,1,0:T(8,128)(2,1)S(1)}, u32[]{:S(2)}, u32[]{:S(2)}) collective-permute-start(bf16[2,2,144,384]{3,2,1,0:T(8,128)(2,1)S(1)} %pad_maximum_fusion.4.pair_pieces), channel_id=1, source_target_pairs={{0,4},{4,0},{8,12},{12,8},{16,20},{20,16},{24,28},{28,24},{1,5},{5... | collective-permute-start | bytes 1327112 | tf_op jit(solution)/shard_map/ppermute | solution.py:46
  182.2 2.8 %collective-permute-start.44 = (bf16[2,2,48,576]{3,2,1,0:T(8,128)(2,1)S(1)}, bf16[2,2,48,576]{3,2,1,0:T(8,128)(2,1)S(1)}, u32[]{:S(2)}, u32[]{:S(2)}) collective-permute-start(bf16[2,2,48,576]{3,2,1,0:T(8,128)(2,1)S(1)} %pad_maximum_fusion.9.down_pieces), channel_id=1, source_target_pairs={{0,4},{4,0},{8,12},{12,8},{16,20},{20,16},{24,28},{28,24},{1,5},{5... | collective-permute-start | bytes 663560 | tf_op jit(solution)/shard_map/ppermute | solution.py:46
  (1 other events, 0.9 us)
where the time goes:
time: 191 us; the launch traced here: 188 us
  waiting for transfers between devices  68.6 us (36%)
  Pallas kernels  55.8 us (29%)
  starting transfers between devices  48.5 us (25%)
  local copies, waits for them, and re-layouts  11.1 us (6%)
  other arithmetic  2.94 us (2%)
    pallas_call x12, Pallas kernels, call(): pl.pallas_call(kernel, name=name, in_specs=in_specs, out_shape=out_shape,...  55.8 us
    ppermute x27, waiting for transfers between devices, flip(): lax.ppermute(value, 'rep', [(i, i ^ 1 << bit) for i in range(replicas)])  48.8 us
    ppermute x27, starting transfers between devices, flip(): lax.ppermute(value, 'rep', [(i, i ^ 1 << bit) for i in range(replicas)])  21 us
    ppermute x9, starting transfers between devices, shift_from(): lax.ppermute(value, 'shard', [((s + step) % shards, s) for s in range(sha...  16.1 us
    ppermute x9, waiting for transfers between devices, shift_to(): lax.ppermute(value, 'shard', [(s, (s + step) % shards) for s in range(sha...  11.6 us
    ppermute x9, starting transfers between devices, shift_to(): lax.ppermute(value, 'shard', [(s, (s + step) % shards) for s in range(sha...  11.3 us
    ppermute x9, waiting for transfers between devices, shift_from(): lax.ppermute(value, 'shard', [((s + step) % shards, s) for s in range(sha...  8.31 us
    unnamed x40, local copies, waits for them, and re-layouts  7.46 us
  transfers between devices with their start and end apart: 45, of which 21 were waited for; matrix products, arithmetic and copies ran while one was open for 2% of the time, Pallas kernels for 12%

commit v1 on v0

--- a/solution.py
+++ b/solution.py
@@ -58,21 +58,21 @@
     return (left.astype(f32) + right.astype(f32)).astype(low)
 
 
-def gather(mine, order, shards, replicas):
-    got = jnp.stack([shift_from(mine, step, shards) for step in range(1, shards)])
-    for bit in order[:-1]:
-        got = jnp.stack([got, flip(got, bit, replicas)])
-    return got, flip(got, order[-1], replicas)
-
-
-def scatter_in_plane(keep, send, order, replicas):
-    other = flip(send, order[0], replicas)
-    for bit in order[1:]:
-        send = add_low(keep[1], other[1])
-        moved = flip(send, bit, replicas)
-        keep = add_low(keep[0], other[0])
-        other = moved
-    return keep, other
+def after(value, *others):
+    return lax.optimization_barrier((value, *others))[0]
+
+
+def gather_shards(mine, shards):
+    return jnp.stack([shift_from(mine, step, shards) for step in range(1, shards)])
+
+
+def gather_bit(got, bit, replicas):
+    return jnp.stack([got, flip(got, bit, replicas)])
+
+
+def halve(keep, other, bit, replicas):
+    sent = flip(add_low(keep[1], other[1]), bit, replicas)
+    return add_low(keep[0], other[0]), sent
 
 
 def scatter_over_shards(keep, other, shards, replicas):
@@ -145,14 +145,11 @@
 
 
 def prepare_kernel(
-    where_ref,
     lengths,
     tokens_t,
     cotangent_t,
     table_cos,
     table_sin,
-    gate,
-    up,
     down_t,
     cosine,
     sine,
@@ -160,17 +157,9 @@
     hidden,
     scaled,
     grad_low,
-    pair_mine,
-    down_mine,
     down,
 ):
-    core, x, y = (where_ref[i] for i in range(3))
-    block = 2 * core + x
-    columns = rows_at(384 * block, 384, 128)
-    pair_mine[...] = jnp.where(y == 0, gate[:, columns], up[:, columns])
     down[...] = down_t[...].T
-    eighth = down_mine.shape[0]
-    down_mine[...] = down[rows_at(eighth * (2 * block + y), eighth), :]
     rows = hidden.shape[0]
     count = lengths.shape[1]
     ends = []
@@ -622,7 +611,7 @@
         out_specs=out_specs,
         scratch_shapes=scratch,
         cost_estimate=pl.CostEstimate(
-            flops=int(micros * 1.1e9), bytes_accessed=moved, transcendentals=0
+            flops=int(micros * 1e7), bytes_accessed=moved, transcendentals=0
         ),
         compiler_params=pltpu.CompilerParams(vmem_limit_bytes=room << 20),
     )(*operands)
@@ -669,13 +658,21 @@
         axis=0,
     )
     attn_mine = lax.dynamic_slice(own, (80 * y, 384 * block), (80, 384))
-    attn_got, attn_other = gather(attn_mine, (2, 1, 0), shards, replicas)
+    pair_mine = jnp.where(
+        y == 0,
+        lax.dynamic_slice(w_gate, (0, 384 * block), (part, 384)),
+        lax.dynamic_slice(w_up, (0, 384 * block), (part, 384)),
+    )
+    down_mine = lax.dynamic_slice(w_down, (eighth * (2 * block + y), 0), (eighth, width))
+    pair_got = gather_shards(pair_mine, shards)
+    down_got = gather_shards(down_mine, shards)
+    attn_got = gather_shards(attn_mine, shards)
     table_cos, table_sin = rotation_tables(rows + 8, HD)
-    cosine, sine, bias, hidden_in, scaled, grad_low, pair_mine, down_mine, own_down = call(
+    cosine, sine, bias, hidden_in, scaled, grad_low, own_down = call(
         prepare_kernel,
         "prepare",
-        (where, lengths, tokens.T, cotangent.T, table_cos, table_sin, w_gate, w_up, w_down.T),
-        [SM, SM] + [VM] * 7,
+        (lengths, tokens.T, cotangent.T, table_cos, table_sin, w_down.T),
+        [SM] + [VM] * 5,
         (
             shape((rows, 2 * HD), f32),
             shape((rows, 2 * HD), f32),
@@ -683,17 +680,21 @@
             shape((rows, width), f32),
             shape((rows, width), f32),
             shape((rows, width), low),
-            shape((part, 384), low),
-            shape((eighth, width), low),
             shape((down_part, width), low),
         ),
-        [VM] * 9,
+        [VM] * 7,
         [],
         5,
         24,
     )
-    pair_got, pair_other = gather(pair_mine, (2, 1, 0), shards, replicas)
-    down_got, down_other = gather(down_mine, (1, 2, 0), shards, replicas)
+    attn_got = after(attn_got, pair_got, down_got, scaled)
+    pair_got = gather_bit(pair_got, 2, replicas)
+    down_got = gather_bit(down_got, 1, replicas)
+    attn_got = gather_bit(gather_bit(attn_got, 2, replicas), 1, replicas)
+    attn_got = after(attn_got, pair_got, down_got)
+    attn_other = flip(attn_got, 0, replicas)
+    pair_got = gather_bit(after(pair_got, attn_other), 1, replicas)
+    down_got = gather_bit(after(down_got, attn_other), 2, replicas)
 
     weights, gains, normed, query, keys, values = call(
         functools.partial(project_kernel, shards, part),
@@ -730,7 +731,7 @@
                 24,
             )
         else:
-            operands += (hidden_in, gains, weights, *mixed)
+            operands += (after(hidden_in, down_got), gains, weights, *mixed)
             one, two, hidden_one, normed_two = call(
                 functools.partial(attend_last_kernel, kv),
                 f"attend_{kv}",
@@ -744,6 +745,8 @@
             )
         mixed.append(one)
         log_total.append(two)
+    pair_other = flip(after(pair_got, normed_two), 0, replicas)
+    down_other = flip(after(down_got, normed_two), 0, replicas)
     pair_shape = shape((2, 2, shards, part, 384), low)
     down_shape = shape((2, 2, shards, eighth, width), low)
     result, grad_one, grad_gain_two, pair_keep, pair_send, down_keep, down_send = call(
@@ -788,8 +791,14 @@
         19,
         48,
     )
+    pair_sent = flip(pair_send, 0, replicas)
+    down_sent = flip(down_send, 0, replicas)
     grad_turned, grad_values, grad_out = [], [], []
     for kv in range(KV):
+        if kv == 1:
+            pair_left = halve(pair_keep, after(pair_sent, grad_turned[0]), 1, replicas)
+            down_left = halve(down_keep, down_sent, 2, replicas)
+            grad_one = after(grad_one, pair_sent, down_sent)
         one, two, three = call(
             functools.partial(back_heads_kernel, kv),
             f"back_{kv}",
@@ -808,6 +817,7 @@
         grad_turned.append(one)
         grad_values.append(two)
         grad_out.append(three)
+    grad_one = after(grad_one, down_left[1])
     attn_shape = shape((2, 2, shards, 80, 384), low)
     grad_tokens, attn_keep, attn_send = call(
         functools.partial(back_last_kernel, shards, part),
@@ -835,15 +845,13 @@
         6,
         24,
     )
-    pair_total = scatter_over_shards(
-        *scatter_in_plane(pair_keep, pair_send, (0, 1, 2), replicas), shards, replicas
-    )
-    down_total = scatter_over_shards(
-        *scatter_in_plane(down_keep, down_send, (0, 2, 1), replicas), shards, replicas
-    )
-    attn_total = scatter_over_shards(
-        *scatter_in_plane(attn_keep, attn_send, (0, 2, 1), replicas), shards, replicas
-    )
+    pair_left = halve(*pair_left, 2, replicas)
+    pair_total = scatter_over_shards(*pair_left, shards, replicas)
+    down_left = halve(*down_left, 1, replicas)
+    down_total = scatter_over_shards(*down_left, shards, replicas)
+    attn_left = halve(attn_keep, flip(attn_send, 0, replicas), 2, replicas)
+    attn_left = halve(*attn_left, 1, replicas)
+    attn_total = scatter_over_shards(*attn_left, shards, replicas)
     g_gate, g_up, g_down = call(
         finish_feed_kernel,
         "finish_feed",

time: 191 us -> 190 us (level)
  local copies, waits for them, and re-layouts: 11.1 us -> 7.01 us
  waiting for transfers between devices: 68.6 us -> 71.4 us
  other arithmetic: 2.94 us -> 5.54 us
  starting transfers between devices: 48.5 us -> 46.3 us
    ppermute x27, waiting for transfers between devices: 48.8 us -> 56.8 us  [flip(): lax.ppermute(value, 'rep', [(i, i ^ 1 << bit) for i in range(replicas)])]
    unnamed x40 -> x31, local copies, waits for them, and re-layouts: 7.46 us -> 1.9 us
    ppermute x9, waiting for transfers between devices: 8.31 us -> 4.88 us  [shift_from(): lax.ppermute(value, 'shard', [((s + step) % shards, s) for s in range(sha...]
  transfers between devices with their start and end apart: 45 -> 45, of which waited for: 21 -> 24; matrix products, arithmetic and copies ran while one was open for 2% -> 5% of each run, Pallas kernels for 12% -> 15%
where the time goes in v1:
time: 190 us; the launch traced here: 187 us
  waiting for transfers between devices  71.4 us (38%)
  Pallas kernels  55.7 us (29%)
  starting transfers between devices  46.3 us (24%)
  local copies, waits for them, and re-layouts  7.01 us (4%)
  other arithmetic  5.54 us (3%)
    ppermute x27, waiting for transfers between devices, flip(): lax.ppermute(value, 'rep', [(i, i ^ 1 << bit) for i in range(replicas)])  56.8 us
    pallas_call x12, Pallas kernels, call(): pl.pallas_call(kernel, name=name, in_specs=in_specs, out_shape=out_shape,...  55.7 us
    ppermute x27, starting transfers between devices, flip(): lax.ppermute(value, 'rep', [(i, i ^ 1 << bit) for i in range(replicas)])  20.9 us
    ppermute x9, starting transfers between devices, shift_from(): lax.ppermute(value, 'shard', [((s + step) % shards, s) for s in range(sha...  15.1 us
    ppermute x9, starting transfers between devices, shift_to(): lax.ppermute(value, 'shard', [(s, (s + step) % shards) for s in range(sha...  10.2 us
    ppermute x9, waiting for transfers between devices, shift_to(): lax.ppermute(value, 'shard', [(s, (s + step) % shards) for s in range(sha...  9.72 us
    ppermute x9, waiting for transfers between devices, shift_from(): lax.ppermute(value, 'shard', [((s + step) % shards, s) for s in range(sha...  4.88 us
  transfers between devices with their start and end apart: 45, of which 24 were waited for; matrix products, arithmetic and copies ran while one was open for 5% of the time, Pallas kernels for 15%

profile of v1, /device:TPU:0, one launch (start us, length us, event | category | flops | bytes accessed | tf_op | source)
XLA Modules:
  0.0 187.4 jit_solution(12854449307092969774)
XLA Ops:
  0.7 1.1 dynamic-slice_select_fusion
  1.9 3.1 %collective-permute-start.5 = (bf16[144,384]{1,0:T(8,128)(2,1)S(1)}, bf16[144,384]{1,0:T(8,128)(2,1)S(1)}, u32[]{:S(2)}, u32[]{:S(2)}) collective-permute-start(bf16[144,384]{1,0:T(8,128)(2,1)S(1)} %dynamic-slice_select_fusion), channel_id=1, source_target_pairs={{3,0},{0,1},{1,2},{2,3},{7,4},{4,5},{5,6},{6,7},{11,8},{8,9},{9,10... | collective-permute-start | bytes 331784 | tf_op jit(solution)/shard_map/ppermute | solution.py:50
  4.9 2.6 %collective-permute-start.4 = (bf16[144,384]{1,0:T(8,128)(2,1)S(1)}, bf16[144,384]{1,0:T(8,128)(2,1)S(1)}, u32[]{:S(2)}, u32[]{:S(2)}) collective-permute-start(bf16[144,384]{1,0:T(8,128)(2,1)S(1)} %dynamic-slice_select_fusion), channel_id=1, source_target_pairs={{2,0},{3,1},{0,2},{1,3},{6,4},{7,5},{4,6},{5,7},{10,8},{11,9},{8,1... | collective-permute-start | bytes 331784 | tf_op jit(solution)/shard_map/ppermute | solution.py:50
  7.5 1.1 constant_dynamic-slice_fusion
  8.6 0.8 copy.26
  9.4 1.8 collective-permute-start.7
  11.3 1.9 %collective-permute-start.6 = (bf16[48,576]{1,0:T(8,128)(2,1)}, bf16[48,576]{1,0:T(8,128)(2,1)}, u32[]{:S(2)}, u32[]{:S(2)}) collective-permute-start(bf16[48,576]{1,0:T(8,128)(2,1)} %copy.26), channel_id=1, source_target_pairs={{1,0},{2,1},{3,2},{0,3},{5,4},{6,5},{7,6},{4,7},{9,8},{10,9},{11,1... | collective-permute-start | bytes 165896 | tf_op jit(solution)/shard_map/ppermute | solution.py:50
  13.2 0.7 stack.173
  15.3 1.3 concatenate.6
  16.6 0.8 maximum_maximum_fusion.own
  17.5 1.7 prepare.1
  19.2 0.7 collective-permute-start.2
  19.9 1.5 collective-permute-start.1
  21.5 2.8 %collective-permute-start = (bf16[80,384]{1,0:T(8,128)(2,1)S(1)}, bf16[80,384]{1,0:T(8,128)(2,1)S(1)}, u32[]{:S(2)}, u32[]{:S(2)}) collective-permute-start(bf16[80,384]{1,0:T(8,128)(2,1)S(1)} %dynamic_slice.15), channel_id=1, source_target_pairs={{1,0},{2,1},{3,2},{0,3},{5,4},{6,5},{7,6},{4,7},{9,8},{10,9},{11,1... | collective-permute-start | bytes 184328 | tf_op jit(solution)/shard_map/ppermute | solution.py:50
  24.3 0.9 fusion.48
  25.9 1.2 collective-permute-done.1
  27.1 3.5 %collective-permute-done.3 = bf16[144,384]{1,0:T(8,128)(2,1)S(1)} collective-permute-done((bf16[144,384]{1,0:T(8,128)(2,1)S(1)}, bf16[144,384]{1,0:T(8,128)(2,1)S(1)}, u32[]{:S(2)}, u32[]{:S(2)}) %collective-permute-start.3) | collective-permute-done | bytes 110624 | tf_op jit(solution)/shard_map/ppermute | solution.py:50
  30.7 1.6 collective-permute-start.9
  32.3 1.5 collective-permute-start.12
  34.3 4.0 %collective-permute-done.9 = bf16[3,80,384]{2,1,0:T(8,128)(2,1)S(1)} collective-permute-done((bf16[3,80,384]{2,1,0:T(8,128)(2,1)S(1)}, bf16[3,80,384]{2,1,0:T(8,128)(2,1)S(1)}, u32[]{:S(2)}, u32[]{:S(2)}) %collective-permute-start.9) | collective-permute-done | bytes 184352 | tf_op jit(solution)/shard_map/ppermute | solution.py:46
  38.3 1.1 collective-permute-start.10
  39.8 2.0 %collective-permute-done.11 = bf16[3,144,384]{2,1,0:T(8,128)(2,1)S(1)} collective-permute-done((bf16[3,144,384]{2,1,0:T(8,128)(2,1)S(1)}, bf16[3,144,384]{2,1,0:T(8,128)(2,1)S(1)}, u32[]{:S(2)}, u32[]{:S(2)}) %collective-permute-start.11) | collective-permute-done | bytes 331808 | tf_op jit(solution)/shard_map/ppermute | solution.py:46
  41.9 4.0 %collective-permute-done.10 = bf16[2,3,80,384]{3,2,1,0:T(8,128)(2,1)S(1)} collective-permute-done((bf16[2,3,80,384]{3,2,1,0:T(8,128)(2,1)S(1)}, bf16[2,3,80,384]{3,2,1,0:T(8,128)(2,1)S(1)}, u32[]{:S(2)}, u32[]{:S(2)}) %collective-permute-start.10) | collective-permute-done | bytes 368672 | tf_op jit(solution)/shard_map/ppermute | solution.py:46
  46.1 2.2 %collective-permute-done.13.other = bf16[2,2,3,80,384]{4,3,2,1,0:T(8,128)(2,1)S(1)} collective-permute-done((bf16[2,2,3,80,384]{4,3,2,1,0:T(8,128)(2,1)S(1)}, bf16[2,2,3,80,384]{4,3,2,1,0:T(8,128)(2,1)S(1)}, u32[]{:S(2)}, u32[]{:S(2)}) %collective-permute-start.13) | collective-permute-done | bytes 737312 | tf_op jit(solution)/shard_map/ppermute | solution.py:46
  48.3 1.0 collective-permute-start.15
  49.3 1.5 collective-permute-start.14
  50.9 3.8 %project.1 = (bf16[640,1536]{1,0:T(8,128)(2,1)S(1)}, f32[8,576]{1,0:T(8,128)S(1)}, bf16[512,576]{1,0:T(8,128)(2,1)S(1)}, bf16[9,512,64]{2,1,0:T(8,128)(2,1)S(1)}...) custom-call(s32[4]{0:T(128)S(1)} %pad_add_fusion.where_ref, f32[512,576]{1,0:T(8,128)S(1)} %get-tuple-element.70.scaled, ...), custom_call_target="tpu_custom_call" | custom-call | flops 50000000 | bytes 3557376 | tf_op jit(solution)/shard_map/project/pallas_call | solution.py:606
  54.7 1.9 %attend_1.1 = (bf16[512,192]{1,0:T(8,128)(2,1)S(1)}, f32[3,512,1]{2,1,0:T(8,128)S(1)}) custom-call(f32[512,512]{1,0:T(8,128)S(1)} %get-tuple-element.69.bias, bf16[9,512,64]{2,1,0:T(8,128)(2,1)S(1)} %get-tuple-element.75.query, bf16[3,512,64]{2,1,0:T(8,128)(2,1)S(1)} %get-tuple-element.76.keys, bf16[3,512,64]{2,1,0:T(8,128)(2,1)S(1)} %get-tuple-element.77.values), custom_call_target="tpu_custom_call" | custom-call | flops 30000000 | bytes 202752 | tf_op jit(solution)/shard_map/attend_1/pallas_call | solution.py:606
  56.6 1.9 %attend_0.1 = (bf16[512,192]{1,0:T(8,128)(2,1)S(1)}, f32[3,512,1]{2,1,0:T(8,128)S(1)}) custom-call(f32[512,512]{1,0:T(8,128)S(1)} %get-tuple-element.69.bias, bf16[9,512,64]{2,1,0:T(8,128)(2,1)S(1)} %get-tuple-element.75.query, bf16[3,512,64]{2,1,0:T(8,128)(2,1)S(1)} %get-tuple-element.76.keys, bf16[3,512,64]{2,1,0:T(8,128)(2,1)S(1)} %get-tuple-element.77.values), custom_call_target="tpu_custom_call" | custom-call | flops 30000000 | bytes 202752 | tf_op jit(solution)/shard_map/attend_0/pallas_call | solution.py:606
  58.5 1.1 collective-permute-done.14
  59.8 2.7 %attend_2.1 = (bf16[512,192]{1,0:T(8,128)(2,1)S(1)}, f32[3,512,1]{2,1,0:T(8,128)S(1)}, f32[512,576]{1,0:T(8,128)S(1)}, bf16[512,576]{1,0:T(8,128)(2,1)S(1)}) custom-call(f32[512,512]{1,0:T(8,128)S(1)} %get-tuple-element.69.bias, bf16[9,512,64]{2,1,0:T(8,128)(2,1)S(1)} %get-tuple-element.75.query, bf16[3,512,64]{2,1,0:T(8,128)(2,1)S(1)} %get-tuple-element.76.keys, ...), custom_call_target="tpu_custom_call" | custom-call | flops 40000000 | bytes 1972224 | tf_op jit(solution)/shard_map/attend_2/pallas_call | solution.py:606
  62.5 2.8 %collective-permute-done.15 = bf16[2,3,144,384]{3,2,1,0:T(8,128)(2,1)S(1)} collective-permute-done((bf16[2,3,144,384]{3,2,1,0:T(8,128)(2,1)S(1)}, bf16[2,3,144,384]{3,2,1,0:T(8,128)(2,1)S(1)}, u32[]{:S(2)}, u32[]{:S(2)}) %collective-permute-start.15) | collective-permute-done | bytes 663584 | tf_op jit(solution)/shard_map/ppermute | solution.py:46
  66.0 3.6 %collective-permute-done.17.down_other = bf16[2,2,3,48,576]{4,3,2,1,0:T(8,128)(2,1)S(1)} collective-permute-done((bf16[2,2,3,48,576]{4,3,2,1,0:T(8,128)(2,1)S(1)}, bf16[2,2,3,48,576]{4,3,2,1,0:T(8,128)(2,1)S(1)}, u32[]{:S(2)}, u32[]{:S(2)}) %collective-permute-start.17) | collective-permute-done | bytes 663584 | tf_op jit(solution)/shard_map/ppermute | solution.py:46
  69.6 1.1 copy-done.14
  70.7 25.1 %feed.1 = (bf16[576,512]{1,0:T(8,128)(2,1)}, f32[512,576]{1,0:T(8,128)}, f32[8,576]{1,0:T(8,128)S(1)}, bf16[2,2,4,144,384]{4,3,2,1,0:T(8,128)(2,1)}, bf16[2,2,4,...) custom-call(s32[4]{0:T(128)S(1)} %pad_add_fusion.where_ref, ...), custom_call_target="tpu_custom_call" | custom-call | flops 190000000 | bytes 7096320 | tf_op jit(solution)/shard_map/feed/pallas_call | solution.py:606
  96.4 4.6 %collective-permute-done.19 = bf16[2,2,4,48,576]{4,3,2,1,0:T(8,128)(2,1)S(1)} collective-permute-done((bf16[2,2,4,48,576]{4,3,2,1,0:T(8,128)(2,1)S(1)}, bf16[2,2,4,48,576]{4,3,2,1,0:T(8,128)(2,1)S(1)}, u32[]{:S(2)}, u32[]{:S(2)}) %collective-permute-start.19) | collective-permute-done | bytes 884768 | tf_op jit(solution)/shard_map/ppermute | solution.py:46
  101.2 1.1 collective-permute-start.20
  102.4 2.9 %back_0.1 = (bf16[512,256]{1,0:T(8,128)(2,1)S(1)}, bf16[512,64]{1,0:T(8,128)(2,1)S(1)}, bf16[192,576]{1,0:T(8,128)(2,1)S(1)}) custom-call(f32[512,512]{1,0:T(8,128)S(1)} %get-tuple-element.69.bias, f32[512,128]{1,0:T(8,128)S(1)} %get-tuple-element.71.cosine, f32[512,128]{1,0:T(8,128)S(1)} %get-tuple-element.72.sine, ...), custom_call_target="tpu_custom_call" | custom-call | flops 50000000 | bytes 548864 | tf_op jit(solution)/shard_map/back_0/pallas_call | solution.py:606
  105.7 1.5 collective-permute-start.30
  107.3 7.3 %collective-permute-done.20 = bf16[2,4,48,576]{3,2,1,0:T(8,128)(2,1)S(1)} collective-permute-done((bf16[2,4,48,576]{3,2,1,0:T(8,128)(2,1)S(1)}, bf16[2,4,48,576]{3,2,1,0:T(8,128)(2,1)S(1)}, u32[]{:S(2)}, u32[]{:S(2)}) %collective-permute-start.20) | collective-permute-done | bytes 442400 | tf_op jit(solution)/shard_map/ppermute | solution.py:46
  114.6 2.9 %back_1.1 = (bf16[512,256]{1,0:T(8,128)(2,1)S(1)}, bf16[512,64]{1,0:T(8,128)(2,1)S(1)}, bf16[192,576]{1,0:T(8,128)(2,1)S(1)}) custom-call(f32[512,512]{1,0:T(8,128)S(1)} %get-tuple-element.69.bias, f32[512,128]{1,0:T(8,128)S(1)} %get-tuple-element.71.cosine, f32[512,128]{1,0:T(8,128)S(1)} %get-tuple-element.72.sine, ...), custom_call_target="tpu_custom_call" | custom-call | flops 50000000 | bytes 548864 | tf_op jit(solution)/shard_map/back_1/pallas_call | solution.py:606
  117.5 3.1 %back_2.1 = (bf16[512,256]{1,0:T(8,128)(2,1)S(1)}, bf16[512,64]{1,0:T(8,128)(2,1)S(1)}, bf16[192,576]{1,0:T(8,128)(2,1)S(1)}) custom-call(f32[512,512]{1,0:T(8,128)S(1)} %get-tuple-element.69.bias, f32[512,128]{1,0:T(8,128)S(1)} %get-tuple-element.71.cosine, f32[512,128]{1,0:T(8,128)S(1)} %get-tuple-element.72.sine, ...), custom_call_target="tpu_custom_call" | custom-call | flops 50000000 | bytes 548864 | tf_op jit(solution)/shard_map/back_2/pallas_call | solution.py:606
  120.6 4.9 %back_last.1 = (bf16[576,512]{1,0:T(8,128)(2,1)}, bf16[2,2,4,80,384]{4,3,2,1,0:T(8,128)(2,1)S(1)}, bf16[2,2,4,80,384]{4,3,2,1,0:T(8,128)(2,1)S(1)}) custom-call(s32[4]{0:T(128)S(1)} %pad_add_fusion.where_ref, f32[512,576]{1,0:T(8,128)S(1)} %get-tuple-element.80.hidden_in, f32[8,576]{1,0:T(8,128)S(1)} %get-tuple-element.81.gains, ...), custom_call_target="tpu_custom_call" | custom-call | flops 60000000 | bytes 2555904 | tf_op jit(solution)/shard_map/back_last/pallas_call | solution.py:606
  125.7 1.1 collective-permute-start.38
  127.4 1.2 collective-permute-start.31
  128.9 0.9 collective-permute-start.22
  129.8 4.3 %collective-permute-done.38 = bf16[4,48,576]{2,1,0:T(8,128)(2,1)S(1)} collective-permute-done((bf16[4,48,576]{2,1,0:T(8,128)(2,1)S(1)}, bf16[4,48,576]{2,1,0:T(8,128)(2,1)S(1)}, u32[]{:S(2)}, u32[]{:S(2)}) %collective-permute-start.38) | collective-permute-done | bytes 221216 | tf_op jit(solution)/shard_map/ppermute | solution.py:46
  134.3 3.8 %collective-permute-start.41 = (bf16[48,576]{1,0:T(8,128)(2,1)S(1)}, bf16[48,576]{1,0:T(8,128)(2,1)S(1)}, u32[]{:S(2)}, u32[]{:S(2)}) collective-permute-start(bf16[48,576]{1,0:T(8,128)(2,1)S(1)} %get-tuple-element.143), channel_id=1, source_target_pairs={{0,3},{1,0},{2,1},{3,2},{4,7},{5,4},{6,5},{7,6},{8,11},{9,8},{10,9... | collective-permute-start | bytes 165896 | tf_op jit(solution)/shard_map/ppermute | solution.py:54
  138.1 2.4 %collective-permute-done.31 = bf16[4,144,384]{2,1,0:T(8,128)(2,1)S(1)} collective-permute-done((bf16[4,144,384]{2,1,0:T(8,128)(2,1)S(1)}, bf16[4,144,384]{2,1,0:T(8,128)(2,1)S(1)}, u32[]{:S(2)}, u32[]{:S(2)}) %collective-permute-start.31) | collective-permute-done | bytes 442400 | tf_op jit(solution)/shard_map/ppermute | solution.py:46
  141.0 8.9 %collective-permute-done.22 = bf16[2,4,80,384]{3,2,1,0:T(8,128)(2,1)S(1)} collective-permute-done((bf16[2,4,80,384]{3,2,1,0:T(8,128)(2,1)S(1)}, bf16[2,4,80,384]{3,2,1,0:T(8,128)(2,1)S(1)}, u32[]{:S(2)}, u32[]{:S(2)}) %collective-permute-start.22) | collective-permute-done | bytes 491552 | tf_op jit(solution)/shard_map/ppermute | solution.py:46
  149.9 2.0 %collective-permute-start.34 = (bf16[144,384]{1,0:T(8,128)(2,1)S(1)}, bf16[144,384]{1,0:T(8,128)(2,1)S(1)}, u32[]{:S(2)}, u32[]{:S(2)}) collective-permute-start(bf16[144,384]{1,0:T(8,128)(2,1)S(1)} %get-tuple-element.140), channel_id=1, source_target_pairs={{0,3},{1,0},{2,1},{3,2},{4,7},{5,4},{6,5},{7,6},{8,11},{9,8},{10,9... | collective-permute-start | bytes 331784 | tf_op jit(solution)/shard_map/ppermute | solution.py:54
  152.1 1.0 collective-permute-start.23
  153.2 1.1 collective-permute-start.42
  154.8 4.4 %collective-permute-done.33 = bf16[144,384]{1,0:T(8,128)(2,1)S(1)} collective-permute-done((bf16[144,384]{1,0:T(8,128)(2,1)S(1)}, bf16[144,384]{1,0:T(8,128)(2,1)S(1)}, u32[]{:S(2)}, u32[]{:S(2)}) %collective-permute-start.33) | collective-permute-done | bytes 110624 | tf_op jit(solution)/shard_map/ppermute | solution.py:54
  159.3 1.6 collective-permute-start.35
  161.5 3.3 %collective-permute-start.26 = (bf16[80,384]{1,0:T(8,128)(2,1)S(1)}, bf16[80,384]{1,0:T(8,128)(2,1)S(1)}, u32[]{:S(2)}, u32[]{:S(2)}) collective-permute-start(bf16[80,384]{1,0:T(8,128)(2,1)S(1)} %get-tuple-element.146), channel_id=1, source_target_pairs={{0,3},{1,0},{2,1},{3,2},{4,7},{5,4},{6,5},{7,6},{8,11},{9,8},{10,9... | collective-permute-start | bytes 184328 | tf_op jit(solution)/shard_map/ppermute | solution.py:54
  165.5 2.1 %collective-permute-done.24 = bf16[80,384]{1,0:T(8,128)(2,1)S(1)} collective-permute-done((bf16[80,384]{1,0:T(8,128)(2,1)S(1)}, bf16[80,384]{1,0:T(8,128)(2,1)S(1)}, u32[]{:S(2)}, u32[]{:S(2)}) %collective-permute-start.24) | collective-permute-done | bytes 61472 | tf_op jit(solution)/shard_map/ppermute | solution.py:54
  167.6 2.7 %collective-permute-done.25 = bf16[80,384]{1,0:T(8,128)(2,1)S(1)} collective-permute-done((bf16[80,384]{1,0:T(8,128)(2,1)S(1)}, bf16[80,384]{1,0:T(8,128)(2,1)S(1)}, u32[]{:S(2)}, u32[]{:S(2)}) %collective-permute-start.25) | collective-permute-done | bytes 61472 | tf_op jit(solution)/shard_map/ppermute | solution.py:54
  171.3 3.4 %collective-permute-done.27 = bf16[80,384]{1,0:T(8,128)(2,1)S(1)} collective-permute-done((bf16[80,384]{1,0:T(8,128)(2,1)S(1)}, bf16[80,384]{1,0:T(8,128)(2,1)S(1)}, u32[]{:S(2)}, u32[]{:S(2)}) %collective-permute-start.27) | collective-permute-done | bytes 61472 | tf_op jit(solution)/shard_map/ppermute | solution.py:46
  174.7 0.7 collective-permute-start.28
  175.5 4.1 %collective-permute-done.28 = bf16[2,80,384]{2,1,0:T(8,128)(2,1)S(1)} collective-permute-done((bf16[2,80,384]{2,1,0:T(8,128)(2,1)S(1)}, bf16[2,80,384]{2,1,0:T(8,128)(2,1)S(1)}, u32[]{:S(2)}, u32[]{:S(2)}) %collective-permute-start.28) | collective-permute-done | bytes 122912 | tf_op jit(solution)/shard_map/ppermute | solution.py:46
  180.3 1.2 collective-permute-done.44.down_other
  181.6 3.2 %finish_feed.1 = (f32[144,1536]{1,0:T(8,128)}, f32[144,1536]{1,0:T(8,128)}, f32[576,384]{1,0:T(8,128)}) custom-call(s32[4]{0:T(128)S(1)} %pad_add_fusion.where_ref, bf16[2,2,144,384]{3,2,1,0:T(8,128)(2,1)S(1)} %pad_maximum_fusion.4.pair_pieces, bf16[2,2,144,384]{3,2,1,0:T(8,128)(2,1)S(1)} %collective-permute-done.37.pair_other, ...), custom_call_target="tpu_custom_call" | custom-call | flops 30000000 | bytes 2654208 | tf_op jit(solution)/shard_map/finish_feed/pallas_call | solution.py:606
  184.8 1.7 finish_attn.1
  (110 shorter events, 12.0 us)
Async XLA Ops:
  0.6 16.8 %copy-start.9 = (f32[520,128]{1,0:T(8,128)S(1)}, f32[520,128]{1,0:T(8,128)}, u32[]{:S(2)}) copy-start(f32[520,128]{1,0:T(8,128)} %constant.37.clone.table_sin) | copy-start | bytes 798724
  0.7 16.8 %copy-start.10 = (f32[520,128]{1,0:T(8,128)S(1)}, f32[520,128]{1,0:T(8,128)}, u32[]{:S(2)}) copy-start(f32[520,128]{1,0:T(8,128)} %constant.36.clone.table_cos) | copy-start | bytes 798724
  0.7 16.8 %copy-start.2 = (bf16[384,576]{0,1:T(8,128)(2,1)S(1)}, bf16[384,576]{0,1:T(8,128)(2,1)}, u32[]{:S(2)}) copy-start(bf16[384,576]{0,1:T(8,128)(2,1)} %param.24) | copy-start | bytes 1327108
  0.7 16.8 %copy-start.11 = (s32[1,4]{1,0:T(1,128)S(1)}, s32[1,4]{1,0:T(1,128)}, u32[]{:S(2)}) copy-start(s32[1,4]{1,0:T(1,128)} %lengths.3) | copy-start | bytes 52
  0.7 16.8 %copy-start.8 = (bf16[512,576]{0,1:T(8,128)(2,1)S(1)}, bf16[512,576]{0,1:T(8,128)(2,1)}, u32[]{:S(2)}) copy-start(bf16[512,576]{0,1:T(8,128)(2,1)} %param.25) | copy-start | bytes 1769476
  0.7 16.8 %copy-start.7 = (bf16[512,576]{0,1:T(8,128)(2,1)S(1)}, bf16[512,576]{0,1:T(8,128)(2,1)}, u32[]{:S(2)}) copy-start(bf16[512,576]{0,1:T(8,128)(2,1)} %param.14) | copy-start | bytes 1769476
  1.9 25.3 %collective-permute-start.5 = (bf16[144,384]{1,0:T(8,128)(2,1)S(1)}, bf16[144,384]{1,0:T(8,128)(2,1)S(1)}, u32[]{:S(2)}, u32[]{:S(2)}) collective-permute-start(bf16[144,384]{1,0:T(8,128)(2,1)S(1)} %dynamic-slice_select_fusion), channel_id=1, source_target_pairs={{3,0},{0,1},{1,2},{2,3},{7,4},{4,5},{5,6},{6,7},{11,8},{8,9},{9,10... | collective-permute-start | bytes 331784 | tf_op jit(solution)/shard_map/ppermute | solution.py:50
  4.9 22.2 %collective-permute-start.4 = (bf16[144,384]{1,0:T(8,128)(2,1)S(1)}, bf16[144,384]{1,0:T(8,128)(2,1)S(1)}, u32[]{:S(2)}, u32[]{:S(2)}) collective-permute-start(bf16[144,384]{1,0:T(8,128)(2,1)S(1)} %dynamic-slice_select_fusion), channel_id=1, source_target_pairs={{2,0},{3,1},{0,2},{1,3},{6,4},{7,5},{4,6},{5,7},{10,8},{11,9},{8,1... | collective-permute-start | bytes 331784 | tf_op jit(solution)/shard_map/ppermute | solution.py:50
  9.3 9.8 %collective-permute-start.8 = (bf16[48,576]{1,0:T(8,128)(2,1)}, bf16[48,576]{1,0:T(8,128)(2,1)S(1)}, u32[]{:S(2)}, u32[]{:S(2)}) collective-permute-start(bf16[48,576]{1,0:T(8,128)(2,1)} %copy.26), channel_id=1, source_target_pairs={{3,0},{0,1},{1,2},{2,3},{7,4},{4,5},{5,6},{6,7},{11,8},{8,9},{9,10... | collective-permute-start | bytes 165896 | tf_op jit(solution)/shard_map/ppermute | solution.py:50
  9.4 10.5 %collective-permute-start.7 = (bf16[48,576]{1,0:T(8,128)(2,1)}, bf16[48,576]{1,0:T(8,128)(2,1)S(1)}, u32[]{:S(2)}, u32[]{:S(2)}) collective-permute-start(bf16[48,576]{1,0:T(8,128)(2,1)} %copy.26), channel_id=1, source_target_pairs={{2,0},{3,1},{0,2},{1,3},{6,4},{7,5},{4,6},{5,7},{10,8},{11,9},{8,1... | collective-permute-start | bytes 165896 | tf_op jit(solution)/shard_map/ppermute | solution.py:50
  11.3 10.2 %collective-permute-start.6 = (bf16[48,576]{1,0:T(8,128)(2,1)}, bf16[48,576]{1,0:T(8,128)(2,1)}, u32[]{:S(2)}, u32[]{:S(2)}) collective-permute-start(bf16[48,576]{1,0:T(8,128)(2,1)} %copy.26), channel_id=1, source_target_pairs={{1,0},{2,1},{3,2},{0,3},{5,4},{6,5},{7,6},{4,7},{9,8},{10,9},{11,1... | collective-permute-start | bytes 165896 | tf_op jit(solution)/shard_map/ppermute | solution.py:50
  19.2 6.2 %collective-permute-start.2 = (bf16[80,384]{1,0:T(8,128)(2,1)S(1)}, bf16[80,384]{1,0:T(8,128)(2,1)S(1)}, u32[]{:S(2)}, u32[]{:S(2)}) collective-permute-start(bf16[80,384]{1,0:T(8,128)(2,1)S(1)} %dynamic_slice.15), channel_id=1, source_target_pairs={{3,0},{0,1},{1,2},{2,3},{7,4},{4,5},{5,6},{6,7},{11,8},{8,9},{9,10... | collective-permute-start | bytes 184328 | tf_op jit(solution)/shard_map/ppermute | solution.py:50
  19.9 7.2 %collective-permute-start.1 = (bf16[80,384]{1,0:T(8,128)(2,1)S(1)}, bf16[80,384]{1,0:T(8,128)(2,1)S(1)}, u32[]{:S(2)}, u32[]{:S(2)}) collective-permute-start(bf16[80,384]{1,0:T(8,128)(2,1)S(1)} %dynamic_slice.15), channel_id=1, source_target_pairs={{2,0},{3,1},{0,2},{1,3},{6,4},{7,5},{4,6},{5,7},{10,8},{11,9},{8,1... | collective-permute-start | bytes 184328 | tf_op jit(solution)/shard_map/ppermute | solution.py:50
  21.5 5.6 %collective-permute-start = (bf16[80,384]{1,0:T(8,128)(2,1)S(1)}, bf16[80,384]{1,0:T(8,128)(2,1)S(1)}, u32[]{:S(2)}, u32[]{:S(2)}) collective-permute-start(bf16[80,384]{1,0:T(8,128)(2,1)S(1)} %dynamic_slice.15), channel_id=1, source_target_pairs={{1,0},{2,1},{3,2},{0,3},{5,4},{6,5},{7,6},{4,7},{9,8},{10,9},{11,1... | collective-permute-start | bytes 184328 | tf_op jit(solution)/shard_map/ppermute | solution.py:50
  25.4 5.3 %collective-permute-start.3 = (bf16[144,384]{1,0:T(8,128)(2,1)S(1)}, bf16[144,384]{1,0:T(8,128)(2,1)S(1)}, u32[]{:S(2)}, u32[]{:S(2)}) collective-permute-start(bf16[144,384]{1,0:T(8,128)(2,1)S(1)} %dynamic-slice_select_fusion), channel_id=1, source_target_pairs={{1,0},{2,1},{3,2},{0,3},{5,4},{6,5},{7,6},{4,7},{9,8},{10,9},{11,1... | collective-permute-start | bytes 331784 | tf_op jit(solution)/shard_map/ppermute | solution.py:50
  30.7 7.6 %collective-permute-start.9 = (bf16[3,80,384]{2,1,0:T(8,128)(2,1)S(1)}, bf16[3,80,384]{2,1,0:T(8,128)(2,1)S(1)}, u32[]{:S(2)}, u32[]{:S(2)}) collective-permute-start(bf16[3,80,384]{2,1,0:T(8,128)(2,1)S(1)} %pad_maximum_fusion.11), channel_id=1, source_target_pairs={{0,16},{4,20},{8,24},{12,28},{16,0},{20,4},{24,8},{28,12},{1,17},{... | collective-permute-start | bytes 552968 | tf_op jit(solution)/shard_map/ppermute | solution.py:46
  32.3 7.5 %collective-permute-start.12 = (bf16[3,48,576]{2,1,0:T(8,128)(2,1)S(1)}, bf16[3,48,576]{2,1,0:T(8,128)(2,1)S(1)}, u32[]{:S(2)}, u32[]{:S(2)}) collective-permute-start(bf16[3,48,576]{2,1,0:T(8,128)(2,1)S(1)} %get-tuple-element.155), channel_id=1, source_target_pairs={{0,8},{4,12},{8,0},{12,4},{16,24},{20,28},{24,16},{28,20},{1,9},{5... | collective-permute-start | bytes 497672 | tf_op jit(solution)/shard_map/ppermute | solution.py:46
  33.8 8.0 %collective-permute-start.11 = (bf16[3,144,384]{2,1,0:T(8,128)(2,1)S(1)}, bf16[3,144,384]{2,1,0:T(8,128)(2,1)S(1)}, u32[]{:S(2)}, u32[]{:S(2)}) collective-permute-start(bf16[3,144,384]{2,1,0:T(8,128)(2,1)S(1)} %get-tuple-element.151), channel_id=1, source_target_pairs={{0,16},{4,20},{8,24},{12,28},{16,0},{20,4},{24,8},{28,12},{1,17},{... | collective-permute-start | bytes 995336 | tf_op jit(solution)/shard_map/ppermute | solution.py:46
  38.3 7.6 %collective-permute-start.10 = (bf16[2,3,80,384]{3,2,1,0:T(8,128)(2,1)S(1)}, bf16[2,3,80,384]{3,2,1,0:T(8,128)(2,1)S(1)}, u32[]{:S(2)}, u32[]{:S(2)}) collective-permute-start(bf16[2,3,80,384]{3,2,1,0:T(8,128)(2,1)S(1)} %get-tuple-element.149), channel_id=1, source_target_pairs={{0,8},{4,12},{8,0},{12,4},{16,24},{20,28},{24,16},{28,20},{1,9},{5... | collective-permute-start | bytes 1105928 | tf_op jit(solution)/shard_map/ppermute | solution.py:46
  46.0 2.3 %collective-permute-start.13 = (bf16[2,2,3,80,384]{4,3,2,1,0:T(8,128)(2,1)S(1)}, bf16[2,2,3,80,384]{4,3,2,1,0:T(8,128)(2,1)S(1)}, u32[]{:S(2)}, u32[]{:S(2)}) collective-permute-start(bf16[2,2,3,80,384]{4,3,2,1,0:T(8,128)(2,1)S(1)} %pad_maximum_fusion.1.pieces), channel_id=1, source_target_pairs={{0,4},{4,0},{8,12},{12,8},{16,20},{20,16},{24,28},{28,24},{1,5},{5... | collective-permute-start | bytes 2211848 | tf_op jit(solution)/shard_map/ppermute | solution.py:46
  48.3 16.9 %collective-permute-start.15 = (bf16[2,3,144,384]{3,2,1,0:T(8,128)(2,1)S(1)}, bf16[2,3,144,384]{3,2,1,0:T(8,128)(2,1)S(1)}, u32[]{:S(2)}, u32[]{:S(2)}) collective-permute-start(bf16[2,3,144,384]{3,2,1,0:T(8,128)(2,1)S(1)} %pad_maximum_fusion.3), channel_id=1, source_target_pairs={{0,8},{4,12},{8,0},{12,4},{16,24},{20,28},{24,16},{28,20},{1,9},{5... | collective-permute-start | bytes 1990664 | tf_op jit(solution)/shard_map/ppermute | solution.py:46
  49.3 10.3 %collective-permute-start.14 = (bf16[2,3,48,576]{3,2,1,0:T(8,128)(2,1)S(1)}, bf16[2,3,48,576]{3,2,1,0:T(8,128)(2,1)S(1)}, u32[]{:S(2)}, u32[]{:S(2)}) collective-permute-start(bf16[2,3,48,576]{3,2,1,0:T(8,128)(2,1)S(1)} %pad_maximum_fusion.6), channel_id=1, source_target_pairs={{0,16},{4,20},{8,24},{12,28},{16,0},{20,4},{24,8},{28,12},{1,17},{... | collective-permute-start | bytes 995336 | tf_op jit(solution)/shard_map/ppermute | solution.py:46
  54.6 3.8 %copy-start.5 = (bf16[512,576]{1,0:T(8,128)(2,1)}, bf16[512,576]{1,0:T(8,128)(2,1)S(1)}, u32[]{:S(2)}) copy-start(bf16[512,576]{1,0:T(8,128)(2,1)S(1)} %get-tuple-element.93.normed) | copy-start | bytes 1769476
  62.4 7.1 %copy-start.1 = (f32[512,576]{1,0:T(8,128)}, f32[512,576]{1,0:T(8,128)S(1)}, u32[]{:S(2)}) copy-start(f32[512,576]{1,0:T(8,128)S(1)} %get-tuple-element.85.hidden_one) | copy-start | bytes 3538948
  62.4 8.2 %copy-start.3 = (bf16[144,1536]{1,0:T(8,128)(2,1)S(1)}, bf16[144,1536]{1,0:T(8,128)(2,1)}, u32[]{:S(2)}) copy-start(bf16[144,1536]{1,0:T(8,128)(2,1)} %own_gate.1) | copy-start | bytes 1327108
  62.4 8.2 %copy-start.4 = (bf16[144,1536]{1,0:T(8,128)(2,1)S(1)}, bf16[144,1536]{1,0:T(8,128)(2,1)}, u32[]{:S(2)}) copy-start(bf16[144,1536]{1,0:T(8,128)(2,1)} %own_up.1) | copy-start | bytes 1327108
  65.4 4.2 %copy-start.12 = (bf16[2,2,3,144,384]{4,3,2,1,0:T(8,128)(2,1)}, bf16[2,2,3,144,384]{4,3,2,1,0:T(8,128)(2,1)S(1)}, u32[]{:S(2)}) copy-start(bf16[2,2,3,144,384]{4,3,2,1,0:T(8,128)(2,1)S(1)} %pad_maximum_fusion.pair_pieces) | copy-start | bytes 3981316
  65.4 4.2 %collective-permute-start.16 = (bf16[2,2,3,144,384]{4,3,2,1,0:T(8,128)(2,1)S(1)}, bf16[2,2,3,144,384]{4,3,2,1,0:T(8,128)(2,1)S(1)}, u32[]{:S(2)}, u32[]{:S(2)}) collective-permute-start(bf16[2,2,3,144,384]{4,3,2,1,0:T(8,128)(2,1)S(1)} %pad_maximum_fusion.pair_pieces), channel_id=1, source_target_pairs={{0,4},{4,0},{8,12},{12,8},{16,20},{20,16},{24,28},{28,24},{1,5},{5... | collective-permute-start | bytes 3981320 | tf_op jit(solution)/shard_map/ppermute | solution.py:46
  65.5 4.1 %collective-permute-start.17 = (bf16[2,2,3,48,576]{4,3,2,1,0:T(8,128)(2,1)S(1)}, bf16[2,2,3,48,576]{4,3,2,1,0:T(8,128)(2,1)S(1)}, u32[]{:S(2)}, u32[]{:S(2)}) collective-permute-start(bf16[2,2,3,48,576]{4,3,2,1,0:T(8,128)(2,1)S(1)} %pad_maximum_fusion.2.down_pieces), channel_id=1, source_target_pairs={{0,4},{4,0},{8,12},{12,8},{16,20},{20,16},{24,28},{28,24},{1,5},{5... | collective-permute-start | bytes 1990664 | tf_op jit(solution)/shard_map/ppermute | solution.py:46
  69.6 1.1 copy-start.14
  95.8 6.5 %copy-start = (f32[512,576]{1,0:T(8,128)S(1)}, f32[512,576]{1,0:T(8,128)}, u32[]{:S(2)}) copy-start(f32[512,576]{1,0:T(8,128)} %get-tuple-element.99.grad_one) | copy-start | bytes 3538948
  95.8 9.4 %collective-permute-start.18 = (bf16[2,2,4,144,384]{4,3,2,1,0:T(8,128)(2,1)}, bf16[2,2,4,144,384]{4,3,2,1,0:T(8,128)(2,1)S(1)}, u32[]{:S(2)}, u32[]{:S(2)}) collective-permute-start(bf16[2,2,4,144,384]{4,3,2,1,0:T(8,128)(2,1)} %get-tuple-element.95), channel_id=1, source_target_pairs={{0,4},{4,0},{8,12},{12,8},{16,20},{20,16},{24,28},{28,24},{1,5},{5... | collective-permute-start | bytes 5308424 | tf_op jit(solution)/shard_map/ppermute | solution.py:46
  96.0 5.0 %collective-permute-start.19 = (bf16[2,2,4,48,576]{4,3,2,1,0:T(8,128)(2,1)S(1)}, bf16[2,2,4,48,576]{4,3,2,1,0:T(8,128)(2,1)S(1)}, u32[]{:S(2)}, u32[]{:S(2)}) collective-permute-start(bf16[2,2,4,48,576]{4,3,2,1,0:T(8,128)(2,1)S(1)} %get-tuple-element.96), channel_id=1, source_target_pairs={{0,4},{4,0},{8,12},{12,8},{16,20},{20,16},{24,28},{28,24},{1,5},{5... | collective-permute-start | bytes 2654216 | tf_op jit(solution)/shard_map/ppermute | solution.py:46
  101.2 13.3 %collective-permute-start.20 = (bf16[2,4,48,576]{3,2,1,0:T(8,128)(2,1)S(1)}, bf16[2,4,48,576]{3,2,1,0:T(8,128)(2,1)S(1)}, u32[]{:S(2)}, u32[]{:S(2)}) collective-permute-start(bf16[2,4,48,576]{3,2,1,0:T(8,128)(2,1)S(1)} %get-tuple-element.130), channel_id=1, source_target_pairs={{0,16},{4,20},{8,24},{12,28},{16,0},{20,4},{24,8},{28,12},{1,17},{... | collective-permute-start | bytes 1327112 | tf_op jit(solution)/shard_map/ppermute | solution.py:46
  102.3 2.9 %copy-start.13 = (bf16[2,2,4,144,384]{4,3,2,1,0:T(8,128)(2,1)S(1)}, bf16[2,2,4,144,384]{4,3,2,1,0:T(8,128)(2,1)}, u32[]{:S(2)}) copy-start(bf16[2,2,4,144,384]{4,3,2,1,0:T(8,128)(2,1)} %get-tuple-element.122) | copy-start | bytes 5308420
  105.7 21.5 %collective-permute-start.30 = (bf16[2,4,144,384]{3,2,1,0:T(8,128)(2,1)S(1)}, bf16[2,4,144,384]{3,2,1,0:T(8,128)(2,1)S(1)}, u32[]{:S(2)}, u32[]{:S(2)}) collective-permute-start(bf16[2,4,144,384]{3,2,1,0:T(8,128)(2,1)S(1)} %get-tuple-element.128), channel_id=1, source_target_pairs={{0,8},{4,12},{8,0},{12,4},{16,24},{20,28},{24,16},{28,20},{1,9},{5... | collective-permute-start | bytes 2654216 | tf_op jit(solution)/shard_map/ppermute | solution.py:46
  117.4 3.1 %copy-start.6 = (bf16[512,576]{1,0:T(8,128)(2,1)S(1)}, bf16[512,576]{1,0:T(8,128)(2,1)}, u32[]{:S(2)}) copy-start(bf16[512,576]{1,0:T(8,128)(2,1)} %copy-done.5) | copy-start | bytes 1769476
  125.5 3.1 %collective-permute-start.21 = (bf16[2,2,4,80,384]{4,3,2,1,0:T(8,128)(2,1)S(1)}, bf16[2,2,4,80,384]{4,3,2,1,0:T(8,128)(2,1)S(1)}, u32[]{:S(2)}, u32[]{:S(2)}) collective-permute-start(bf16[2,2,4,80,384]{4,3,2,1,0:T(8,128)(2,1)S(1)} %get-tuple-element.116), channel_id=1, source_target_pairs={{0,4},{4,0},{8,12},{12,8},{16,20},{20,16},{24,28},{28,24},{1,5},{5... | collective-permute-start | bytes 2949128 | tf_op jit(solution)/shard_map/ppermute | solution.py:46
  125.7 8.4 %collective-permute-start.38 = (bf16[4,48,576]{2,1,0:T(8,128)(2,1)S(1)}, bf16[4,48,576]{2,1,0:T(8,128)(2,1)S(1)}, u32[]{:S(2)}, u32[]{:S(2)}) collective-permute-start(bf16[4,48,576]{2,1,0:T(8,128)(2,1)S(1)} %get-tuple-element.136), channel_id=1, source_target_pairs={{0,8},{4,12},{8,0},{12,4},{16,24},{20,28},{24,16},{28,20},{1,9},{5... | collective-permute-start | bytes 663560 | tf_op jit(solution)/shard_map/ppermute | solution.py:46
  127.4 13.1 %collective-permute-start.31 = (bf16[4,144,384]{2,1,0:T(8,128)(2,1)S(1)}, bf16[4,144,384]{2,1,0:T(8,128)(2,1)S(1)}, u32[]{:S(2)}, u32[]{:S(2)}) collective-permute-start(bf16[4,144,384]{2,1,0:T(8,128)(2,1)S(1)} %get-tuple-element.134), channel_id=1, source_target_pairs={{0,16},{4,20},{8,24},{12,28},{16,0},{20,4},{24,8},{28,12},{1,17},{... | collective-permute-start | bytes 1327112 | tf_op jit(solution)/shard_map/ppermute | solution.py:46
  128.9 21.0 %collective-permute-start.22 = (bf16[2,4,80,384]{3,2,1,0:T(8,128)(2,1)S(1)}, bf16[2,4,80,384]{3,2,1,0:T(8,128)(2,1)S(1)}, u32[]{:S(2)}, u32[]{:S(2)}) collective-permute-start(bf16[2,4,80,384]{3,2,1,0:T(8,128)(2,1)S(1)} %get-tuple-element.132), channel_id=1, source_target_pairs={{0,16},{4,20},{8,24},{12,28},{16,0},{20,4},{24,8},{28,12},{1,17},{... | collective-permute-start | bytes 1474568 | tf_op jit(solution)/shard_map/ppermute | solution.py:46
  134.2 17.8 %collective-permute-start.39 = (bf16[48,576]{1,0:T(8,128)(2,1)S(1)}, bf16[48,576]{1,0:T(8,128)(2,1)S(1)}, u32[]{:S(2)}, u32[]{:S(2)}) collective-permute-start(bf16[48,576]{1,0:T(8,128)(2,1)S(1)} %get-tuple-element.142), channel_id=1, source_target_pairs={{0,1},{1,2},{2,3},{3,0},{4,5},{5,6},{6,7},{7,4},{8,9},{9,10},{10,1... | collective-permute-start | bytes 165896 | tf_op jit(solution)/shard_map/ppermute | solution.py:54
  134.3 17.8 %collective-permute-start.41 = (bf16[48,576]{1,0:T(8,128)(2,1)S(1)}, bf16[48,576]{1,0:T(8,128)(2,1)S(1)}, u32[]{:S(2)}, u32[]{:S(2)}) collective-permute-start(bf16[48,576]{1,0:T(8,128)(2,1)S(1)} %get-tuple-element.143), channel_id=1, source_target_pairs={{0,3},{1,0},{2,1},{3,2},{4,7},{5,4},{6,5},{7,6},{8,11},{9,8},{10,9... | collective-permute-start | bytes 165896 | tf_op jit(solution)/shard_map/ppermute | solution.py:54
  138.1 15.0 %collective-permute-start.40 = (bf16[48,576]{1,0:T(8,128)(2,1)S(1)}, bf16[48,576]{1,0:T(8,128)(2,1)S(1)}, u32[]{:S(2)}, u32[]{:S(2)}) collective-permute-start(bf16[48,576]{1,0:T(8,128)(2,1)S(1)} %get-tuple-element.144), channel_id=1, source_target_pairs={{0,2},{1,3},{2,0},{3,1},{4,6},{5,7},{6,4},{7,5},{8,10},{9,11},{10,... | collective-permute-start | bytes 165896 | tf_op jit(solution)/shard_map/ppermute | solution.py:54
  140.6 13.7 %collective-permute-start.32 = (bf16[144,384]{1,0:T(8,128)(2,1)S(1)}, bf16[144,384]{1,0:T(8,128)(2,1)S(1)}, u32[]{:S(2)}, u32[]{:S(2)}) collective-permute-start(bf16[144,384]{1,0:T(8,128)(2,1)S(1)} %get-tuple-element.139), channel_id=1, source_target_pairs={{0,1},{1,2},{2,3},{3,0},{4,5},{5,6},{6,7},{7,4},{8,9},{9,10},{10,1... | collective-permute-start | bytes 331784 | tf_op jit(solution)/shard_map/ppermute | solution.py:54
  149.9 4.9 %collective-permute-start.34 = (bf16[144,384]{1,0:T(8,128)(2,1)S(1)}, bf16[144,384]{1,0:T(8,128)(2,1)S(1)}, u32[]{:S(2)}, u32[]{:S(2)}) collective-permute-start(bf16[144,384]{1,0:T(8,128)(2,1)S(1)} %get-tuple-element.140), channel_id=1, source_target_pairs={{0,3},{1,0},{2,1},{3,2},{4,7},{5,4},{6,5},{7,6},{8,11},{9,8},{10,9... | collective-permute-start | bytes 331784 | tf_op jit(solution)/shard_map/ppermute | solution.py:54
  152.0 7.2 %collective-permute-start.33 = (bf16[144,384]{1,0:T(8,128)(2,1)S(1)}, bf16[144,384]{1,0:T(8,128)(2,1)S(1)}, u32[]{:S(2)}, u32[]{:S(2)}) collective-permute-start(bf16[144,384]{1,0:T(8,128)(2,1)S(1)} %get-tuple-element.141), channel_id=1, source_target_pairs={{0,2},{1,3},{2,0},{3,1},{4,6},{5,7},{6,4},{7,5},{8,10},{9,11},{10,... | collective-permute-start | bytes 331784 | tf_op jit(solution)/shard_map/ppermute | solution.py:54
  152.1 8.8 %collective-permute-start.23 = (bf16[4,80,384]{2,1,0:T(8,128)(2,1)S(1)}, bf16[4,80,384]{2,1,0:T(8,128)(2,1)S(1)}, u32[]{:S(2)}, u32[]{:S(2)}) collective-permute-start(bf16[4,80,384]{2,1,0:T(8,128)(2,1)S(1)} %get-tuple-element.138), channel_id=1, source_target_pairs={{0,8},{4,12},{8,0},{12,4},{16,24},{20,28},{24,16},{28,20},{1,9},{5... | collective-permute-start | bytes 737288 | tf_op jit(solution)/shard_map/ppermute | solution.py:46
  153.2 17.5 %collective-permute-start.42 = (bf16[48,576]{1,0:T(8,128)(2,1)S(1)}, bf16[48,576]{1,0:T(8,128)(2,1)S(1)}, u32[]{:S(2)}, u32[]{:S(2)}) collective-permute-start(bf16[48,576]{1,0:T(8,128)(2,1)S(1)} %fusion.27), channel_id=1, source_target_pairs={{0,8},{4,12},{8,0},{12,4},{16,24},{20,28},{24,16},{28,20},{1,9},{5... | collective-permute-start | bytes 165896 | tf_op jit(solution)/shard_map/ppermute | solution.py:46
  159.3 5.6 %collective-permute-start.35 = (bf16[144,384]{1,0:T(8,128)(2,1)S(1)}, bf16[144,384]{1,0:T(8,128)(2,1)S(1)}, u32[]{:S(2)}, u32[]{:S(2)}) collective-permute-start(bf16[144,384]{1,0:T(8,128)(2,1)S(1)} %fusion.19), channel_id=1, source_target_pairs={{0,16},{4,20},{8,24},{12,28},{16,0},{20,4},{24,8},{28,12},{1,17},{... | collective-permute-start | bytes 331784 | tf_op jit(solution)/shard_map/ppermute | solution.py:46
  160.9 6.6 %collective-permute-start.24 = (bf16[80,384]{1,0:T(8,128)(2,1)S(1)}, bf16[80,384]{1,0:T(8,128)(2,1)S(1)}, u32[]{:S(2)}, u32[]{:S(2)}) collective-permute-start(bf16[80,384]{1,0:T(8,128)(2,1)S(1)} %get-tuple-element.145), channel_id=1, source_target_pairs={{0,1},{1,2},{2,3},{3,0},{4,5},{5,6},{6,7},{7,4},{8,9},{9,10},{10,1... | collective-permute-start | bytes 184328 | tf_op jit(solution)/shard_map/ppermute | solution.py:54
  161.5 6.1 %collective-permute-start.26 = (bf16[80,384]{1,0:T(8,128)(2,1)S(1)}, bf16[80,384]{1,0:T(8,128)(2,1)S(1)}, u32[]{:S(2)}, u32[]{:S(2)}) collective-permute-start(bf16[80,384]{1,0:T(8,128)(2,1)S(1)} %get-tuple-element.146), channel_id=1, source_target_pairs={{0,3},{1,0},{2,1},{3,2},{4,7},{5,4},{6,5},{7,6},{8,11},{9,8},{10,9... | collective-permute-start | bytes 184328 | tf_op jit(solution)/shard_map/ppermute | solution.py:54
  164.8 5.5 %collective-permute-start.25 = (bf16[80,384]{1,0:T(8,128)(2,1)S(1)}, bf16[80,384]{1,0:T(8,128)(2,1)S(1)}, u32[]{:S(2)}, u32[]{:S(2)}) collective-permute-start(bf16[80,384]{1,0:T(8,128)(2,1)S(1)} %get-tuple-element.147), channel_id=1, source_target_pairs={{0,2},{1,3},{2,0},{3,1},{4,6},{5,7},{6,4},{7,5},{8,10},{9,11},{10,... | collective-permute-start | bytes 184328 | tf_op jit(solution)/shard_map/ppermute | solution.py:54
  164.9 10.4 %collective-permute-start.36 = (bf16[2,144,384]{2,1,0:T(8,128)(2,1)S(1)}, bf16[2,144,384]{2,1,0:T(8,128)(2,1)S(1)}, u32[]{:S(2)}, u32[]{:S(2)}) collective-permute-start(bf16[2,144,384]{2,1,0:T(8,128)(2,1)S(1)} %get-tuple-element.153), channel_id=1, source_target_pairs={{0,8},{4,12},{8,0},{12,4},{16,24},{20,28},{24,16},{28,20},{1,9},{5... | collective-permute-start | bytes 663560 | tf_op jit(solution)/shard_map/ppermute | solution.py:46
  170.4 4.3 %collective-permute-start.27 = (bf16[80,384]{1,0:T(8,128)(2,1)S(1)}, bf16[80,384]{1,0:T(8,128)(2,1)S(1)}, u32[]{:S(2)}, u32[]{:S(2)}) collective-permute-start(bf16[80,384]{1,0:T(8,128)(2,1)S(1)} %fusion.35), channel_id=1, source_target_pairs={{0,8},{4,12},{8,0},{12,4},{16,24},{20,28},{24,16},{28,20},{1,9},{5... | collective-permute-start | bytes 184328 | tf_op jit(solution)/shard_map/ppermute | solution.py:46
  170.7 9.1 %collective-permute-start.43 = (bf16[2,48,576]{2,1,0:T(8,128)(2,1)S(1)}, bf16[2,48,576]{2,1,0:T(8,128)(2,1)S(1)}, u32[]{:S(2)}, u32[]{:S(2)}) collective-permute-start(bf16[2,48,576]{2,1,0:T(8,128)(2,1)S(1)} %get-tuple-element.157), channel_id=1, source_target_pairs={{0,16},{4,20},{8,24},{12,28},{16,0},{20,4},{24,8},{28,12},{1,17},{... | collective-permute-start | bytes 331784 | tf_op jit(solution)/shard_map/ppermute | solution.py:46
  174.7 4.9 %collective-permute-start.28 = (bf16[2,80,384]{2,1,0:T(8,128)(2,1)S(1)}, bf16[2,80,384]{2,1,0:T(8,128)(2,1)S(1)}, u32[]{:S(2)}, u32[]{:S(2)}) collective-permute-start(bf16[2,80,384]{2,1,0:T(8,128)(2,1)S(1)} %get-tuple-element.159), channel_id=1, source_target_pairs={{0,16},{4,20},{8,24},{12,28},{16,0},{20,4},{24,8},{28,12},{1,17},{... | collective-permute-start | bytes 368648 | tf_op jit(solution)/shard_map/ppermute | solution.py:46
  175.4 6.2 %collective-permute-start.37 = (bf16[2,2,144,384]{3,2,1,0:T(8,128)(2,1)S(1)}, bf16[2,2,144,384]{3,2,1,0:T(8,128)(2,1)S(1)}, u32[]{:S(2)}, u32[]{:S(2)}) collective-permute-start(bf16[2,2,144,384]{3,2,1,0:T(8,128)(2,1)S(1)} %pad_maximum_fusion.4.pair_pieces), channel_id=1, source_target_pairs={{0,4},{4,0},{8,12},{12,8},{16,20},{20,16},{24,28},{28,24},{1,5},{5... | collective-permute-start | bytes 1327112 | tf_op jit(solution)/shard_map/ppermute | solution.py:46
  179.6 5.1 %collective-permute-start.29 = (bf16[2,2,80,384]{3,2,1,0:T(8,128)(2,1)S(1)}, bf16[2,2,80,384]{3,2,1,0:T(8,128)(2,1)S(1)}, u32[]{:S(2)}, u32[]{:S(2)}) collective-permute-start(bf16[2,2,80,384]{3,2,1,0:T(8,128)(2,1)S(1)} %pad_maximum_fusion.8.pieces), channel_id=1, source_target_pairs={{0,4},{4,0},{8,12},{12,8},{16,20},{20,16},{24,28},{28,24},{1,5},{5... | collective-permute-start | bytes 737288 | tf_op jit(solution)/shard_map/ppermute | solution.py:46
  179.8 1.8 collective-permute-start.44
